TPU v7x, 256 devices: a whole 4x4x8 slice. The times are simulated.
256 devices in a mesh: blk: 64 (over z, y, x_lo), off: 4 (over x_hi, core).
Axes of the slice: x: 4 (x_hi: 2, x_lo: 2; x = x_hi * 2 + x_lo), y: 4, z: 8, core: 2. Of those that a mesh axis runs over, the one named last changes fastest.
Arguments:
- traces: bfloat16 [64, 4, 1024, 2048], P('blk', 'off'), may hold values from -6 to 6
- tables: bfloat16 [64, 128, 2, 2048], P('blk'), may hold values from 0 to 7, as said below
- band_start: int32 [64, 4, 5, 1024], P('blk', 'off'), may hold values from 0 to 2032
- src_station: int32 [64], replicated, may hold values from 0 to 127
- rec_station: int32 [64, 4, 1024], P(None, 'off'), may hold values from 0 to 127
- aperture: int32 [64, 5], replicated, may hold values from 0 to 63, as said below
- aperture_weight: float32 [64, 5], replicated, may hold values from 0.5 to 1.5
Outputs:
- image_out: float32 [64, 2048], P('blk')
Inputs may be any that keep to these rules, and one draw needn't show every extreme that they name: `aperture`: each row b lists 5 distinct tile ids: b itself, (b - 3) and (b + 3) modulo 64, and others within 3 positions of b around the closed cycle of 64 tiles, in any order. `tables`: index 0 holds traveltimes from 0 to 7 samples, index 1 amplitudes from 0.25 to 2.
All inputs are finite; a program needn't handle non-finite values.
Results may differ from a plain program's by a relative error of at most 0.0003.
Values may be sent and summed in bfloat16 or wider, within the bound.
A program may use at most 128 MiB of HBM per device.

v0:
```python
import math

import jax
import jax.numpy as jnp
from jax import lax
from jax.sharding import PartitionSpec as P

BW = 16
APER = 5
HALF = 3


def shifted(x, axis, by):
    devices = lax.axis_size(axis)
    return lax.ppermute(x, axis, [(i, (i + by) % devices) for i in range(devices)])


def take_bands(trace_rows, starts):
    rows = trace_rows.shape[0]
    samples = trace_rows.shape[1]
    width = math.gcd(samples, 128)
    count = samples // width
    blocked = trace_rows.reshape(rows, count, width)
    padded = jnp.concatenate([blocked, jnp.zeros((rows, 1, width), trace_rows.dtype)], axis=1)
    block_ids = jnp.arange(count + 1, dtype=jnp.int32)
    window_pos = jnp.arange(2 * width, dtype=jnp.int32)
    tap_range = jnp.arange(BW, dtype=jnp.int32)
    result = []
    for slot_number in range(starts.shape[0]):
        quotient = starts[slot_number] // width
        remainder = starts[slot_number] % width
        lower_mask = (block_ids[None, :] == quotient[:, None])[:, :, None]
        upper_mask = (block_ids[None, :] == quotient[:, None] + 1)[:, :, None]
        lower = jnp.sum(jnp.where(lower_mask, padded, 0.0), axis=1, dtype=jnp.float32)
        upper = jnp.sum(jnp.where(upper_mask, padded, 0.0), axis=1, dtype=jnp.float32)
        window = jnp.concatenate([lower, upper], axis=1)
        pick_mask = (
            window_pos[None, None, :] == (remainder[:, None] + tap_range[None, :])[:, :, None]
        )
        band = jnp.sum(jnp.where(pick_mask, window[:, None, :], 0.0), axis=2)
        result.append(band.T.astype(jnp.bfloat16))
    return jnp.stack(result)


def migrate(trace_band, source_id, receivers, tile_table):
    stations = tile_table.shape[0]
    points = tile_table.shape[2]
    flat_table = tile_table.reshape(stations, 2 * points)
    onehot = (receivers[:, None] == jnp.arange(stations, dtype=jnp.int32)[None, :]).astype(
        jnp.bfloat16
    )
    receiver_vals = jnp.dot(onehot, flat_table, preferred_element_type=jnp.float32)
    source_vals = lax.dynamic_index_in_dim(flat_table, source_id, 0, keepdims=False).astype(
        jnp.float32
    )
    arrival = source_vals[None, :points] + receiver_vals[:, :points]
    weight = source_vals[None, points:] * receiver_vals[:, points:]
    samples = trace_band.astype(jnp.float32)
    interp = jnp.zeros(arrival.shape, jnp.float32)
    for tap_number in range(trace_band.shape[0]):
        interp = (
            interp
            + jnp.maximum(0.0, 1.0 - jnp.abs(arrival - tap_number)) * samples[tap_number][:, None]
        )
    return jnp.sum(weight * interp, axis=0)


def shards(traces, tables, band_start, src_station, rec_station, aperture, aperture_weight):
    tiles = lax.axis_size("blk")
    groups = lax.axis_size("off")
    my_block = lax.axis_index("blk")
    trace_rows = traces[0, 0]
    bands = take_bands(trace_rows, band_start[0, 0])
    own_table = tables[0]
    receivers = rec_station[:, 0, :]
    points = own_table.shape[2]
    norm_scale = 1.0 / math.sqrt(trace_rows.shape[0] * groups * APER)
    stacked = []
    for offset in range(-HALF, HALF + 1):
        if offset == 0:
            stacked.append(own_table)
        else:
            stacked.append(shifted(own_table, "blk", -offset))
    near_stack = jnp.stack(stacked)
    slot_rows = jnp.arange(2 * HALF + 1, dtype=jnp.int32)[:, None]
    partials = jnp.zeros((2 * HALF + 1, points), jnp.float32)
    for slot_number in range(APER):
        target = aperture[my_block, slot_number]
        position = (target - my_block + HALF) % tiles
        chosen_table = lax.dynamic_index_in_dim(near_stack, position, 0, keepdims=False)
        term_value = aperture_weight[my_block, slot_number] * migrate(
            bands[slot_number], src_station[my_block], receivers[my_block], chosen_table
        )
        partials = partials + jnp.where(slot_rows == position, term_value[None, :], 0.0)
    accumulated = partials[HALF]
    for offset in range(-HALF, HALF + 1):
        if offset != 0:
            accumulated = accumulated + shifted(partials[offset + HALF], "blk", offset)
    image_sum = lax.psum(accumulated, "off") * norm_scale
    return image_sum[None, :]


def solution(mesh):
    placed = (
        P("blk", "off", None, None),
        P("blk", None, None, None),
        P("blk", "off", None, None),
        P(),
        P(None, "off", None),
        P(),
        P(),
    )
    return jax.shard_map(
        shards, mesh=mesh, in_specs=placed, out_specs=P("blk", None), check_vma=False
    )
```

profile of v0, /device:TPU:1, one launch (start us, length us, event | category | flops | bytes accessed | tf_op | source)
XLA Modules:
  0.0 479.5 jit_solution(16690273494372218024)
XLA Ops:
  0.0 10.0 %collective-permute-start.5 = (bf16[128,2,2048]{2,1,0:T(2,128)(2,1)}, bf16[128,2,2048]{2,1,0:T(2,128)(2,1)}, u32[]{:S(2)}, u32[]{:S(2)}) collective-permute-start(bf16[128,2,2048]{2,1,0:T(2,128)(2,1)} %bitcast.104), channel_id=1, source_target_pairs={{0,244},{4,248},{8,252},{12,0},{16,4},{20,8},{24,12},{28,16},{32,2... | collective-permute-start | bytes 3145736 | tf_op jit(solution)/shard_map/ppermute | solution.py:15
  10.0 0.8 collective-permute-start.4
  11.5 1.4 collective-permute-start
  12.9 1.5 constant_dynamic-slice_fusion.7
  19.2 0.9 iota_compare_fusion.7
  20.0 0.8 iota_compare_fusion.8
  20.9 0.9 iota_compare_fusion.10
  21.7 0.9 iota_compare_fusion.11
  22.6 0.8 iota_compare_fusion.12
  24.5 3.6 copy.9
  28.1 1.0 iota_compare_fusion.13
  29.1 33.4 %convert_reduce_fusion.9 = (f32[1024,128]{1,0:T(8,128)}, f32[1024,128]{1,0:T(8,128)}, f32[1024,128]{1,0:T(8,128)}, f32[1024,128]{1,0:T(8,128)}, f32[1024,128]{1,...) fusion(bf16[1024,16,128]{2,1,0:T(8,128)(2,1)S(1)} %bitcast.82, ...), kind=kLoop, calls=%fused_computation.19 | loop fusion | flops 65536000 | bytes 9611264 | tf_op jit(solution)/shard_map/reduce_sum | solution.py:34
  62.5 1.4 pad_maximum_fusion
  63.9 27.9 %select_reduce_fusion.4 = bf16[1024,16]{1,0:T(8,128)(2,1)S(1)} fusion(f32[1024,256]{1,0:T(8,128)S(1)} %pad_maximum_fusion, s32[1024,16]{1,0:T(8,128)S(1)} %iota_add_fusion.4), kind=kLoop, calls=%fused_computation.8 | loop fusion | flops 12566528 | bytes 1146880 | tf_op jit(solution)/shard_map/reduce_sum | solution.py:40
  91.8 4.3 slice_reduce_fusion.79
  96.2 28.1 %select_reduce_fusion.3 = bf16[1024,16]{1,0:T(8,128)(2,1)S(1)} fusion(f32[1024,256]{1,0:T(8,128)S(1)} %pad_maximum_fusion.1, s32[1024,16]{1,0:T(8,128)S(1)} %iota_add_fusion.3), kind=kLoop, calls=%fused_computation.6 | loop fusion | flops 12566528 | bytes 1146880 | tf_op jit(solution)/shard_map/reduce_sum | solution.py:40
  124.4 4.3 slice_reduce_fusion.63
  128.7 27.9 %select_reduce_fusion.2 = bf16[1024,16]{1,0:T(8,128)(2,1)S(1)} fusion(f32[1024,256]{1,0:T(8,128)S(1)} %pad_maximum_fusion.2, s32[1024,16]{1,0:T(8,128)S(1)} %iota_add_fusion.2), kind=kLoop, calls=%fused_computation.4 | loop fusion | flops 12566528 | bytes 1146880 | tf_op jit(solution)/shard_map/reduce_sum | solution.py:40
  156.7 4.9 %slice_reduce_fusion.47 = (f32[1024]{0:T(1024)S(1)}, f32[1024]{0:T(1024)S(1)}, f32[1024]{0:T(1024)S(1)}, f32[1024]{0:T(1024)}, f32[1024]{0:T(1024)}, /*index=5*/...) fusion(f32[16,1024]{0,1:T(8,128)S(1)} %convert_bitcast_fusion.2), kind=kLoop, calls=%fused_computation.108 | loop fusion | bytes 131072 | tf_op jit(solution)/shard_map/slice | solution.py:63
  162.7 27.9 %select_reduce_fusion.1 = bf16[1024,16]{1,0:T(8,128)(2,1)S(1)} fusion(f32[1024,256]{1,0:T(8,128)S(1)} %pad_maximum_fusion.3, s32[1024,16]{1,0:T(8,128)S(1)} %iota_add_fusion.1), kind=kLoop, calls=%fused_computation.2 | loop fusion | flops 12566528 | bytes 1146880 | tf_op jit(solution)/shard_map/reduce_sum | solution.py:40
  190.7 28.3 %select_reduce_fusion = bf16[1024,16]{1,0:T(8,128)(2,1)S(1)} fusion(f32[1024,256]{1,0:T(8,128)S(1)} %pad_maximum_fusion.4, s32[1024,16]{1,0:T(8,128)S(1)} %iota_add_fusion), kind=kLoop, calls=%fused_computation | loop fusion | flops 12566528 | bytes 1146880 | tf_op jit(solution)/shard_map/reduce_sum | solution.py:40
  219.1 4.3 slice_reduce_fusion.31
  223.4 4.3 slice_reduce_fusion.15
  231.0 4.7 collective-permute-start.3
  235.7 1.9 bitcast_dynamic-update-slice_fusion.5
  237.7 2.0 bitcast_dynamic-update-slice_fusion.4
  239.7 2.0 bitcast_dynamic-update-slice_fusion.3
  241.8 0.8 constant_dynamic-update-slice_fusion
  242.6 13.8 %collective-permute-done.3 = bf16[128,2,2048]{2,1,0:T(2,128)(2,1)S(1)} collective-permute-done((bf16[128,2,2048]{2,1,0:T(2,128)(2,1)S(1)}, bf16[128,2,2048]{2,1,0:T(2,128)(2,1)S(1)}, u32[]{:S(2)}, u32[]{:S(2)}) %collective-permute-start.3) | collective-permute-done | bytes 1048608 | tf_op jit(solution)/shard_map/ppermute | solution.py:15
  256.4 0.8 bitcast_dynamic-update-slice_fusion.2
  257.2 2.0 bitcast_dynamic-update-slice_fusion.1
  259.2 2.0 bitcast_dynamic-update-slice_fusion
  261.3 3.9 constant_dynamic-slice_fusion.5
  266.6 8.1 %fusion.13 = f32[1024,4096]{1,0:T(8,128)} fusion(bf16[128,4096]{1,0:T(8,128)(2,1)S(1)} %bitcast.89, s32[1024]{0:T(1024)S(1)} %bitcast.99), kind=kOutput, calls=%fused_computation.165 | convolution fusion | flops 1073872896 | bytes 17829888 | tf_op jit(solution)/shard_map/dot_general | solution.py:52
  274.7 8.1 %fusion.12 = f32[1024,4096]{1,0:T(8,128)} fusion(bf16[128,4096]{1,0:T(8,128)(2,1)S(1)} %bitcast.87, s32[1024]{0:T(1024)S(1)} %bitcast.100), kind=kOutput, calls=%fused_computation.164 | convolution fusion | flops 1073872896 | bytes 17829888 | tf_op jit(solution)/shard_map/dot_general | solution.py:52
  282.8 8.1 %fusion.11 = f32[1024,4096]{1,0:T(8,128)} fusion(bf16[128,4096]{1,0:T(8,128)(2,1)S(1)} %bitcast.85, s32[1024]{0:T(1024)S(1)} %bitcast.101), kind=kOutput, calls=%fused_computation.163 | convolution fusion | flops 1073872896 | bytes 17829888 | tf_op jit(solution)/shard_map/dot_general | solution.py:52
  291.0 2.4 fusion.10
  293.8 2.4 fusion.14
  296.3 30.0 %fusion.7 = f32[2048]{0:T(1024)S(1)} fusion(f32[1024,4096]{1,0:T(8,128)} %fusion.13, f32[1024]{0:T(1024)S(1)} %get-tuple-element.31, f32[1024]{0:T(1024)S(1)} %get-tuple-element.32, f32[1024]{0:T(1024)S(1)} %get-tuple-element.33, f32[1024]{0:T(1024)S(1)} %get-tuple-element.34, f32[1024]{0:T(1024)S(1)} %get-tuple-element.35, f32[1024]{0:T(1024)S(1)} %get-tuple-element.36, ...), kind=kLoop, calls=%fused_computation.45 | loop fusion | flops 205518848 | bytes 16867328 | tf_op jit(solution)/shard_map/reduce_sum | solution.py:65
  327.0 29.7 %fusion.5 = f32[2048]{0:T(1024)S(1)} fusion(f32[1024,4096]{1,0:T(8,128)} %fusion.12, f32[1024]{0:T(1024)S(1)} %get-tuple-element.47, f32[1024]{0:T(1024)S(1)} %get-tuple-element.48, f32[1024]{0:T(1024)S(1)} %copy-done.6, f32[1024]{0:T(1024)S(1)} %copy-done.7, f32[1024]{0:T(1024)S(1)} %copy-done.8, f32[1024]{0:T(1024)S(1)} %copy-done.9, ...), kind=kLoop, calls=%fused_computation.41 | loop fusion | flops 205518848 | bytes 16867328 | tf_op jit(solution)/shard_map/reduce_sum | solution.py:65
  357.4 29.7 %fusion.3 = f32[2048]{0:T(1024)S(1)} fusion(f32[1024,4096]{1,0:T(8,128)} %fusion.11, f32[1024]{0:T(1024)S(1)} %get-tuple-element.63, f32[1024]{0:T(1024)S(1)} %get-tuple-element.64, f32[1024]{0:T(1024)S(1)} %get-tuple-element.65, f32[1024]{0:T(1024)S(1)} %get-tuple-element.66, f32[1024]{0:T(1024)S(1)} %get-tuple-element.67, f32[1024]{0:T(1024)S(1)} %get-tuple-element.68, ...), kind=kLoop, calls=%fused_computation.37 | loop fusion | flops 205518848 | bytes 16867328 | tf_op jit(solution)/shard_map/reduce_sum | solution.py:65
  387.8 31.1 %fusion.1 = f32[2048]{0:T(1024)S(1)} fusion(f32[1024,4096]{1,0:T(8,128)S(1)} %fusion.10, f32[1024]{0:T(1024)S(1)} %get-tuple-element.79, f32[1024]{0:T(1024)S(1)} %get-tuple-element.80, f32[1024]{0:T(1024)S(1)} %get-tuple-element.81, f32[1024]{0:T(1024)S(1)} %get-tuple-element.82, f32[1024]{0:T(1024)S(1)} %get-tuple-element.83, ...), kind=kLoop, calls=%fused_computation.33 | loop fusion | flops 205518848 | bytes 16867328 | tf_op jit(solution)/shard_map/reduce_sum | solution.py:65
  419.6 31.0 %fusion.9 = f32[2048]{0:T(1024)S(1)} fusion(f32[1024,4096]{1,0:T(8,128)S(1)} %fusion.14, f32[1024]{0:T(1024)S(1)} %get-tuple-element.15, f32[1024]{0:T(1024)S(1)} %get-tuple-element.16, f32[1024]{0:T(1024)S(1)} %get-tuple-element.17, f32[1024]{0:T(1024)S(1)} %get-tuple-element.18, f32[1024]{0:T(1024)S(1)} %get-tuple-element.19, ...), kind=kLoop, calls=%fused_computation.49 | loop fusion | flops 205518848 | bytes 16867328 | tf_op jit(solution)/shard_map/reduce_sum | solution.py:65
  451.6 6.0 %collective-permute-start.6 = (f32[2048]{0:T(1024)S(1)}, f32[2048]{0:T(1024)S(1)}, u32[]{:S(2)}, u32[]{:S(2)}) collective-permute-start(f32[2048]{0:T(1024)S(1)} %bitcast.130), channel_id=1, source_target_pairs={{0,244},{4,248},{8,252},{12,0},{16,4},{20,8},{24,12},{28,16},{32,2... | collective-permute-start | bytes 24584 | tf_op jit(solution)/shard_map/ppermute | solution.py:15
  457.5 1.1 collective-permute-start.10
  458.7 5.7 %collective-permute-start.8 = (f32[2048]{0:T(1024)S(1)}, f32[2048]{0:T(1024)S(1)}, u32[]{:S(2)}, u32[]{:S(2)}) collective-permute-start(f32[2048]{0:T(1024)S(1)} %bitcast.127), channel_id=1, source_target_pairs={{0,252},{4,0},{8,4},{12,8},{16,12},{20,16},{24,20},{28,24},{32,28}... | collective-permute-start | bytes 24584 | tf_op jit(solution)/shard_map/ppermute | solution.py:15
  465.4 1.8 collective-permute-done.7
  467.2 11.3 %psum.7 = f32[2048]{0:T(1024)S(1)} all-reduce(f32[2048]{0:T(1024)S(1)} %add_add_fusion), channel_id=1, replica_groups=mesh['blk'=64,'off'=4] {'off'}, use_global_device_ids=true, to_apply=%region_20.21 | all-reduce | flops 2048 | bytes 16384 | tf_op jit(solution)/shard_map/psum | solution.py:99
  (114 shorter events, 13.1 us)
Async XLA Ops:
  0.0 17.7 %copy-start = (s32[64,1,1024]{2,1,0:T(1,128)S(1)}, s32[64,1,1024]{2,1,0:T(1,128)}, u32[]{:S(2)}) copy-start(s32[64,1,1024]{2,1,0:T(1,128)} %param.11) | copy-start | bytes 786436
  0.0 259.2 %collective-permute-start.5 = (bf16[128,2,2048]{2,1,0:T(2,128)(2,1)}, bf16[128,2,2048]{2,1,0:T(2,128)(2,1)}, u32[]{:S(2)}, u32[]{:S(2)}) collective-permute-start(bf16[128,2,2048]{2,1,0:T(2,128)(2,1)} %bitcast.104), channel_id=1, source_target_pairs={{0,244},{4,248},{8,252},{12,0},{16,4},{20,8},{24,12},{28,16},{32,2... | collective-permute-start | bytes 3145736 | tf_op jit(solution)/shard_map/ppermute | solution.py:15
  10.0 247.2 %collective-permute-start.4 = (bf16[128,2,2048]{2,1,0:T(2,128)(2,1)}, bf16[128,2,2048]{2,1,0:T(2,128)(2,1)}, u32[]{:S(2)}, u32[]{:S(2)}) collective-permute-start(bf16[128,2,2048]{2,1,0:T(2,128)(2,1)} %bitcast.105), channel_id=1, source_target_pairs={{0,248},{4,252},{8,0},{12,4},{16,8},{20,12},{24,16},{28,20},{32,24... | collective-permute-start | bytes 3145736 | tf_op jit(solution)/shard_map/ppermute | solution.py:15
  10.7 229.0 %collective-permute-start.2 = (bf16[128,2,2048]{2,1,0:T(2,128)(2,1)}, bf16[128,2,2048]{2,1,0:T(2,128)(2,1)}, u32[]{:S(2)}, u32[]{:S(2)}) collective-permute-start(bf16[128,2,2048]{2,1,0:T(2,128)(2,1)} %bitcast.106), channel_id=1, source_target_pairs={{0,4},{4,8},{8,12},{12,16},{16,20},{20,24},{24,28},{28,32},{32,36}... | collective-permute-start | bytes 3145736 | tf_op jit(solution)/shard_map/ppermute | solution.py:15
  10.7 227.0 %collective-permute-start.1 = (bf16[128,2,2048]{2,1,0:T(2,128)(2,1)}, bf16[128,2,2048]{2,1,0:T(2,128)(2,1)}, u32[]{:S(2)}, u32[]{:S(2)}) collective-permute-start(bf16[128,2,2048]{2,1,0:T(2,128)(2,1)} %bitcast.107), channel_id=1, source_target_pairs={{0,8},{4,12},{8,16},{12,20},{16,24},{20,28},{24,32},{28,36},{32,40... | collective-permute-start | bytes 3145736 | tf_op jit(solution)/shard_map/ppermute | solution.py:15
  11.5 219.5 %collective-permute-start = (bf16[128,2,2048]{2,1,0:T(2,128)(2,1)}, bf16[128,2,2048]{2,1,0:T(2,128)(2,1)}, u32[]{:S(2)}, u32[]{:S(2)}) collective-permute-start(bf16[128,2,2048]{2,1,0:T(2,128)(2,1)} %bitcast.108), channel_id=1, source_target_pairs={{0,12},{4,16},{8,20},{12,24},{16,28},{20,32},{24,36},{28,40},{32,4... | collective-permute-start | bytes 3145736 | tf_op jit(solution)/shard_map/ppermute | solution.py:15
  62.5 33.6 %copy-start.3 = (f32[1024,128]{1,0:T(8,128)S(1)}, f32[1024,128]{1,0:T(8,128)}, u32[]{:S(2)}) copy-start(f32[1024,128]{1,0:T(8,128)} %get-tuple-element.7) | copy-start | bytes 1572868
  62.5 33.6 %copy-start.4 = (f32[1024,128]{1,0:T(8,128)S(1)}, f32[1024,128]{1,0:T(8,128)}, u32[]{:S(2)}) copy-start(f32[1024,128]{1,0:T(8,128)} %get-tuple-element.8) | copy-start | bytes 1572868
  96.1 32.6 %copy-start.2 = (f32[1024,128]{1,0:T(8,128)S(1)}, f32[1024,128]{1,0:T(8,128)}, u32[]{:S(2)}) copy-start(f32[1024,128]{1,0:T(8,128)} %get-tuple-element.10) | copy-start | bytes 1572868
  219.1 8.6 %copy-start.24 = (s32[64]{0:T(128)S(1)}, s32[64]{0:T(128)}, u32[]{:S(2)}) copy-start(s32[64]{0:T(128)} %param.10) | copy-start | bytes 772
  219.1 11.2 %copy-start.23 = (f32[64,5]{0,1:T(8,128)S(1)}, f32[64,5]{0,1:T(8,128)}, u32[]{:S(2)}) copy-start(f32[64,5]{0,1:T(8,128)} %param.13) | copy-start | bytes 3844
  219.1 11.9 %copy-start.5 = (bf16[1,128,2,2048]{3,2,1,0:T(2,128)(2,1)S(1)}, bf16[1,128,2,2048]{3,2,1,0:T(2,128)(2,1)}, u32[]{:S(2)}) copy-start(bf16[1,128,2,2048]{3,2,1,0:T(2,128)(2,1)} %param.8) | copy-start | bytes 3145732
  231.0 25.4 %collective-permute-start.3 = (bf16[128,2,2048]{2,1,0:T(2,128)(2,1)S(1)}, bf16[128,2,2048]{2,1,0:T(2,128)(2,1)S(1)}, u32[]{:S(2)}, u32[]{:S(2)}) collective-permute-start(bf16[128,2,2048]{2,1,0:T(2,128)(2,1)S(1)} %bitcast.109), channel_id=1, source_target_pairs={{0,252},{4,0},{8,4},{12,8},{16,12},{20,16},{24,20},{28,24},{32,28}... | collective-permute-start | bytes 3145736 | tf_op jit(solution)/shard_map/ppermute | solution.py:15
  296.2 30.7 %copy-start.6 = (f32[1024]{0:T(1024)S(1)}, f32[1024]{0:T(1024)}, u32[]{:S(2)}) copy-start(f32[1024]{0:T(1024)} %get-tuple-element.49) | copy-start | bytes 12292
  296.2 30.7 %copy-start.7 = (f32[1024]{0:T(1024)S(1)}, f32[1024]{0:T(1024)}, u32[]{:S(2)}) copy-start(f32[1024]{0:T(1024)} %get-tuple-element.50) | copy-start | bytes 12292
  296.2 30.7 %copy-start.8 = (f32[1024]{0:T(1024)S(1)}, f32[1024]{0:T(1024)}, u32[]{:S(2)}) copy-start(f32[1024]{0:T(1024)} %get-tuple-element.51) | copy-start | bytes 12292
  296.2 30.7 %copy-start.9 = (f32[1024]{0:T(1024)S(1)}, f32[1024]{0:T(1024)}, u32[]{:S(2)}) copy-start(f32[1024]{0:T(1024)} %get-tuple-element.52) | copy-start | bytes 12292
  296.2 30.7 %copy-start.10 = (f32[1024]{0:T(1024)S(1)}, f32[1024]{0:T(1024)}, u32[]{:S(2)}) copy-start(f32[1024]{0:T(1024)} %get-tuple-element.53) | copy-start | bytes 12292
  296.3 30.7 %copy-start.11 = (f32[1024]{0:T(1024)S(1)}, f32[1024]{0:T(1024)}, u32[]{:S(2)}) copy-start(f32[1024]{0:T(1024)} %get-tuple-element.54) | copy-start | bytes 12292
  296.3 30.7 %copy-start.12 = (f32[1024]{0:T(1024)S(1)}, f32[1024]{0:T(1024)}, u32[]{:S(2)}) copy-start(f32[1024]{0:T(1024)} %get-tuple-element.55) | copy-start | bytes 12292
  296.3 30.7 %copy-start.13 = (f32[1024]{0:T(1024)S(1)}, f32[1024]{0:T(1024)}, u32[]{:S(2)}) copy-start(f32[1024]{0:T(1024)} %get-tuple-element.56) | copy-start | bytes 12292
  296.3 30.7 %copy-start.14 = (f32[1024]{0:T(1024)S(1)}, f32[1024]{0:T(1024)}, u32[]{:S(2)}) copy-start(f32[1024]{0:T(1024)} %get-tuple-element.57) | copy-start | bytes 12292
  296.3 30.7 %copy-start.15 = (f32[1024]{0:T(1024)S(1)}, f32[1024]{0:T(1024)}, u32[]{:S(2)}) copy-start(f32[1024]{0:T(1024)} %get-tuple-element.58) | copy-start | bytes 12292
  296.3 30.7 %copy-start.16 = (f32[1024]{0:T(1024)S(1)}, f32[1024]{0:T(1024)}, u32[]{:S(2)}) copy-start(f32[1024]{0:T(1024)} %get-tuple-element.59) | copy-start | bytes 12292
  296.3 30.7 %copy-start.17 = (f32[1024]{0:T(1024)S(1)}, f32[1024]{0:T(1024)}, u32[]{:S(2)}) copy-start(f32[1024]{0:T(1024)} %get-tuple-element.60) | copy-start | bytes 12292
  296.3 30.7 %copy-start.18 = (f32[1024]{0:T(1024)S(1)}, f32[1024]{0:T(1024)}, u32[]{:S(2)}) copy-start(f32[1024]{0:T(1024)} %get-tuple-element.61) | copy-start | bytes 12292
  419.5 59.5 %copy-start.1 = (s32[64,1,1024]{2,1,0:T(1,128)S(1)}, s32[64,1,1024]{2,1,0:T(1,128)}, u32[]{:S(2)}) copy-start(s32[64,1,1024]{2,1,0:T(1,128)} %param.11) | copy-start | bytes 786436
  419.5 31.8 %copy-start.19 = (pred[7]{0:T(512)(128)(4,1)S(1)}, pred[7]{0:T(512)(128)(4,1)}, u32[]{:S(2)}) copy-start(pred[7]{0:T(512)(128)(4,1)} %get-tuple-element.161) | copy-start | bytes 25
  419.5 31.8 %copy-start.20 = (pred[7]{0:T(512)(128)(4,1)S(1)}, pred[7]{0:T(512)(128)(4,1)}, u32[]{:S(2)}) copy-start(pred[7]{0:T(512)(128)(4,1)} %get-tuple-element.162) | copy-start | bytes 25
  419.5 31.8 %copy-start.21 = (pred[7]{0:T(512)(128)(4,1)S(1)}, pred[7]{0:T(512)(128)(4,1)}, u32[]{:S(2)}) copy-start(pred[7]{0:T(512)(128)(4,1)} %get-tuple-element.159) | copy-start | bytes 25
  419.6 31.8 %copy-start.22 = (pred[7]{0:T(512)(128)(4,1)S(1)}, pred[7]{0:T(512)(128)(4,1)}, u32[]{:S(2)}) copy-start(pred[7]{0:T(512)(128)(4,1)} %get-tuple-element.160) | copy-start | bytes 25
  451.5 12.9 %collective-permute-start.11 = (f32[2048]{0:T(1024)S(1)}, f32[2048]{0:T(1024)S(1)}, u32[]{:S(2)}, u32[]{:S(2)}) collective-permute-start(f32[2048]{0:T(1024)S(1)} %bitcast.131), channel_id=1, source_target_pairs={{0,12},{4,16},{8,20},{12,24},{16,28},{20,32},{24,36},{28,40},{32,4... | collective-permute-start | bytes 24584 | tf_op jit(solution)/shard_map/ppermute | solution.py:15
  451.6 13.1 %collective-permute-start.6 = (f32[2048]{0:T(1024)S(1)}, f32[2048]{0:T(1024)S(1)}, u32[]{:S(2)}, u32[]{:S(2)}) collective-permute-start(f32[2048]{0:T(1024)S(1)} %bitcast.130), channel_id=1, source_target_pairs={{0,244},{4,248},{8,252},{12,0},{16,4},{20,8},{24,12},{28,16},{32,2... | collective-permute-start | bytes 24584 | tf_op jit(solution)/shard_map/ppermute | solution.py:15
  457.5 7.2 %collective-permute-start.10 = (f32[2048]{0:T(1024)S(1)}, f32[2048]{0:T(1024)S(1)}, u32[]{:S(2)}, u32[]{:S(2)}) collective-permute-start(f32[2048]{0:T(1024)S(1)} %bitcast.129), channel_id=1, source_target_pairs={{0,8},{4,12},{8,16},{12,20},{16,24},{20,28},{24,32},{28,36},{32,40... | collective-permute-start | bytes 24584 | tf_op jit(solution)/shard_map/ppermute | solution.py:15
  458.7 6.7 %collective-permute-start.9 = (f32[2048]{0:T(1024)S(1)}, f32[2048]{0:T(1024)S(1)}, u32[]{:S(2)}, u32[]{:S(2)}) collective-permute-start(f32[2048]{0:T(1024)S(1)} %bitcast.128), channel_id=1, source_target_pairs={{0,4},{4,8},{8,12},{12,16},{16,20},{20,24},{24,28},{28,32},{32,36}... | collective-permute-start | bytes 24584 | tf_op jit(solution)/shard_map/ppermute | solution.py:15
  458.7 6.7 %collective-permute-start.8 = (f32[2048]{0:T(1024)S(1)}, f32[2048]{0:T(1024)S(1)}, u32[]{:S(2)}, u32[]{:S(2)}) collective-permute-start(f32[2048]{0:T(1024)S(1)} %bitcast.127), channel_id=1, source_target_pairs={{0,252},{4,0},{8,4},{12,8},{16,12},{20,16},{24,20},{28,24},{32,28}... | collective-permute-start | bytes 24584 | tf_op jit(solution)/shard_map/ppermute | solution.py:15
  464.3 2.8 collective-permute-start.7
where the time goes:
time: 483 us; the launch traced here: 479 us
  other arithmetic  339 us (70%)
  local copies, waits for them, and re-layouts  46.7 us (10%)
  starting transfers between devices  30.9 us (6%)
  matrix products  29 us (6%)
  waiting for transfers between devices  16.3 us (3%)
  blocking collectives  11.3 us (2%)
  between operations  6.52 us (1%)
    reduce_sum x5, other arithmetic, migrate(): return jnp.sum(weight * interp, axis=0)  151 us
    reduce_sum x5, other arithmetic, take_bands(): band = jnp.sum(jnp.where(pick_mask, window[:, None, :], 0.0), axis=2)  140 us
    reduce_sum x1, other arithmetic, take_bands(): jnp.sum(jnp.where(lower_mask, padded, 0.0), axis=1, dtype=jnp.float32)  33.4 us
    ppermute x12, starting transfers between devices, shifted(): lax.ppermute(x, axis, [(i, (i + by) % devices) for i in range(devices)])  30.9 us
    dot_general x5, matrix products, migrate(): jnp.dot(onehot, flat_table, preferred_element_type=jnp.float32)  29 us
    slice x5, local copies, waits for them, and re-layouts, migrate(): samples[tap_number][:, None]  22 us
    ppermute x12, waiting for transfers between devices, shifted(): lax.ppermute(x, axis, [(i, (i + by) % devices) for i in range(devices)])  16.3 us
    unnamed x62, local copies, waits for them, and re-layouts  15.1 us
  transfers between devices with their start and end apart: 12, of which 3 were waited for; matrix products, arithmetic and copies ran while one was open for 46% of the time, Pallas kernels for 0%

commit v1 on v0

v1 whole, which is shorter than its diff:
```python
import functools
import math

import jax
import jax.numpy as jnp
from jax import lax
from jax.experimental import pallas as pl
from jax.experimental.pallas import tpu as pltpu
from jax.sharding import PartitionSpec as P

BW = 16
APER = 5
HALF = 3
NOFF = 2 * HALF + 1
LANES = 128
CHUNKS = 8
STEP = 16
MESH = pl.DeviceIdType.MESH


def lane_take(x, idx):
    return jnp.take_along_axis(x, idx, axis=1, mode="promise_in_bounds")


def kernel(
    tiles, groups, scale,
    traces, tabs, starts, src, rec, aper, aw,
    out,
    trace_v, tabs_v, tab32, starts_v, src_v, rec_v, aper_v, aw_v,
    pos_v, window_v, send_v, recv_v, low_v, slope_v, source_v,
    load_sem, chunk_sem, send_sem, recv_sem, peer_send_sem, peer_recv_sem,
):
    rows, samples = trace_v.shape
    stations = send_v.shape[1]
    blk = lax.axis_index("blk")
    off = lax.axis_index("off")

    def at_tile(d):
        return lax.rem(blk + (d + tiles), tiles)

    barrier = pltpu.get_barrier_semaphore()
    for step in range(1, groups):
        pl.semaphore_signal(
            barrier, inc=1, device_id=(blk, lax.rem(off + step, groups)), device_id_type=MESH
        )

    @pl.when(off > 0)
    def _():
        for sign in (-1, 1):
            for g in range(groups):
                other = lax.rem(blk + sign * off + tiles, tiles)
                pl.semaphore_signal(barrier, inc=1, device_id=(other, g), device_id_type=MESH)

    small = [
        pltpu.make_async_copy(starts, starts_v, load_sem.at[0]),
        pltpu.make_async_copy(aper, aper_v, load_sem.at[1]),
        pltpu.make_async_copy(rec.at[blk], rec_v, load_sem.at[2]),
        pltpu.make_async_copy(aw, aw_v, load_sem.at[3]),
        pltpu.make_async_copy(src, src_v, load_sem.at[4]),
    ]
    for copy in small:
        copy.start()
    per = rows // CHUNKS

    def chunk_copy(i):
        span = pl.ds(pl.multiple_of(i * per, per), per)
        return pltpu.make_async_copy(traces.at[span], trace_v.at[span], chunk_sem.at[i])

    for i in range(CHUNKS):
        chunk_copy(i).start()
    tabs_copy = pltpu.make_async_copy(tabs, tabs_v, load_sem.at[5])
    tabs_copy.start()

    small[0].wait()
    small[1].wait()
    small[3].wait()
    mine = lax.broadcasted_iota(jnp.int32, (APER, tiles), 1) == blk
    target = jnp.sum(jnp.where(mine, aper_v[...], 0), axis=1, keepdims=True)
    taper = jnp.sum(jnp.where(mine, aw_v[...], 0.0), axis=1, keepdims=True)
    place = lax.rem(target - blk + (HALF + tiles), tiles)
    lane_off = lax.broadcasted_iota(jnp.int32, (APER, LANES), 1) // BW
    hit = (lane_off == place).astype(jnp.float32)
    taper_row = jnp.sum(hit * taper, axis=0, keepdims=True)
    begin = starts_v[:, 0, :]
    high = (begin >> 7).astype(jnp.float32)
    low = (begin & (LANES - 1)).astype(jnp.float32)
    fill = jnp.zeros((8 - APER, rows), jnp.float32)
    digits = jnp.concatenate([high, fill, low, fill], axis=0).astype(jnp.bfloat16)
    gap = jnp.zeros((8 - APER, LANES), jnp.float32)
    pick = jnp.concatenate([hit * LANES, gap, hit, gap], axis=0).astype(jnp.bfloat16)
    first = lax.dot_general(
        digits, pick, (((0,), (0,)), ((), ())), preferred_element_type=jnp.float32
    )
    tap = lax.broadcasted_iota(jnp.int32, (rows, LANES), 1) & (BW - 1)
    pos_v[...] = first.astype(jnp.int32) + tap

    def do_chunk(i, carry):
        chunk_copy(i).wait()

        def do_rows(k, inner):
            span = pl.ds(pl.multiple_of(i * per + k * STEP, STEP), STEP)
            pos = pos_v[span, :]
            inside = pos & (LANES - 1)
            block = pos >> 7
            acc = jnp.zeros((STEP, LANES), jnp.float32)
            for c in range(samples // LANES):
                piece = trace_v[span, c * LANES:(c + 1) * LANES].astype(jnp.float32)
                acc = jnp.where(block == c, lane_take(piece, inside), acc)
            window_v[span, :] = acc.astype(jnp.bfloat16)
            return inner

        return lax.fori_loop(0, per // STEP, do_rows, carry)

    lax.fori_loop(0, CHUNKS, do_chunk, 0)

    small[2].wait()
    onehot = (
        lax.broadcasted_iota(jnp.int32, (stations, rows), 0) == rec_v[...]
    ).astype(jnp.float32).astype(jnp.bfloat16)
    sums = jnp.dot(onehot, window_v[...], preferred_element_type=jnp.float32) * taper_row
    send_v[...] = sums.T

    pl.semaphore_wait(barrier, groups - 1 + 2 * HALF)

    def band_copy(d):
        slot = 1 if d > 0 else 0
        o = d + HALF
        return pltpu.make_async_remote_copy(
            src_ref=send_v.at[pl.ds(o * BW, BW)],
            dst_ref=recv_v.at[slot, off],
            send_sem=send_sem.at[o],
            recv_sem=recv_sem.at[slot, off],
            device_id=(at_tile(d), abs(d)),
            device_id_type=MESH,
        )

    def band_wait(slot, g):
        pltpu.make_async_remote_copy(
            src_ref=send_v.at[pl.ds(0, BW)],
            dst_ref=recv_v.at[slot, g],
            send_sem=send_sem.at[0],
            recv_sem=recv_sem.at[slot, g],
            device_id=(blk, off),
            device_id_type=MESH,
        ).wait_recv()

    for d in (-3, 3, -2, 2, -1, 1):
        band_copy(d).start()

    @pl.when(off > 0)
    def _():
        band_copy(0).start()

    @pl.when(off == 0)
    def _():
        recv_v[0, 0] = send_v[HALF * BW:(HALF + 1) * BW, :]
        recv_v[1] = jnp.zeros(recv_v.shape[1:], jnp.float32)

    tabs_copy.wait()
    small[4].wait()
    cols = tab32.shape[0] // stations // 2
    origins = (at_tile(off), lax.rem(blk - off + tiles, tiles))
    lane = lax.broadcasted_iota(jnp.int32, (1, tiles), 1)
    source_ids = [
        jnp.sum(jnp.where(lane == origin, src_v[...], 0), axis=1, keepdims=True)
        for origin in origins
    ]

    def widen(r, rows_of):
        span = pl.ds(pl.multiple_of(r * (2 * cols), 2 * cols), 2 * cols)
        wide = tabs_v[span, :].astype(jnp.float32)
        tab32[span, :] = wide
        return tuple(jnp.where(i == r, wide, old) for i, old in zip(source_ids, rows_of))

    blank = jnp.zeros((2 * cols, LANES), jnp.float32)
    found = lax.fori_loop(0, stations, widen, (blank, blank), unroll=4)
    source_v[0] = found[0]
    source_v[1] = found[1]

    for g in range(groups):
        if g == 0:
            @pl.when(off > 0)
            def _():
                band_wait(0, 0)
        else:
            band_wait(0, g)

    @pl.when(off > 0)
    def _():
        for g in range(groups):
            band_wait(1, g)

    base = []
    slope = []
    tap_id = lax.broadcasted_iota(jnp.int32, (BW, stations), 0).astype(jnp.float32)
    for slot in range(2):
        total = (recv_v[slot, 0] + recv_v[slot, 1]) + (recv_v[slot, 2] + recv_v[slot, 3])
        after = jnp.concatenate([total[1:], total[BW - 1:]], axis=0)
        step = after - total
        base.append(total - tap_id * step)
        slope.append(step)
    rest = jnp.zeros((LANES - 2 * BW, stations), jnp.float32)
    low_v[...] = jnp.concatenate(base + [rest], axis=0).T
    slope_v[...] = jnp.concatenate(slope + [rest], axis=0).T

    sources = [
        (source_v[slot, pl.ds(0, cols, stride=2), :], source_v[slot, pl.ds(1, cols, stride=2), :])
        for slot in range(2)
    ]

    def do_station(r, acc):
        row = pl.multiple_of(r * (2 * cols), 2 * cols)
        time = tab32[pl.ds(row, cols, stride=2), :]
        amp = tab32[pl.ds(row + 1, cols, stride=2), :]
        base_row = jnp.broadcast_to(low_v[pl.ds(r, 1), :], (cols, LANES))
        slope_row = jnp.broadcast_to(slope_v[pl.ds(r, 1), :], (cols, LANES))
        result = []
        for slot in range(2):
            arrival = sources[slot][0] + time
            cell = arrival.astype(jnp.int32) + BW * slot
            value = lane_take(base_row, cell) + lane_take(slope_row, cell) * arrival
            result.append(acc[slot] + amp * value)
        return tuple(result)

    zero = jnp.zeros((cols, LANES), jnp.float32)
    acc = lax.fori_loop(0, stations, do_station, (zero, zero), unroll=4)
    out[off] = (sources[0][1] * acc[0] + sources[1][1] * acc[1]) * scale

    def peer_copy(step):
        return pltpu.make_async_remote_copy(
            src_ref=out.at[off],
            dst_ref=out.at[off],
            send_sem=peer_send_sem.at[step - 1],
            recv_sem=peer_recv_sem.at[off],
            device_id=(blk, lax.rem(off + step, groups)),
            device_id_type=MESH,
        )

    for step in range(1, groups):
        peer_copy(step).start()
    for step in range(1, groups):
        other = lax.rem(off + step, groups)
        pltpu.make_async_remote_copy(
            src_ref=out.at[off],
            dst_ref=out.at[other],
            send_sem=peer_send_sem.at[step - 1],
            recv_sem=peer_recv_sem.at[other],
            device_id=(blk, other),
            device_id_type=MESH,
        ).wait_recv()
    for d in (-3, 3, -2, 2, -1, 1):
        band_copy(d).wait_send()

    @pl.when(off > 0)
    def _():
        band_copy(0).wait_send()

    for step in range(1, groups):
        peer_copy(step).wait_send()


def shards(traces, tables, band_start, src_vtation, rec_station, aperture, aperture_weight):
    tiles = lax.axis_size("blk")
    groups = lax.axis_size("off")
    rows, samples = traces.shape[2:]
    stations, _, points = tables.shape[1:]
    cols = points // LANES
    tabs = tables.reshape(stations, 2, cols, LANES).transpose(0, 2, 1, 3)
    tabs = tabs.reshape(stations * cols * 2, LANES)
    scale = 1.0 / math.sqrt(rows * groups * APER)
    any_spec = pl.BlockSpec(memory_space=pltpu.HBM)
    parts = pl.pallas_call(
        functools.partial(kernel, tiles, groups, scale),
        out_shape=jax.ShapeDtypeStruct((groups, cols, LANES), jnp.float32),
        in_specs=[any_spec] * 7,
        out_specs=pl.BlockSpec(memory_space=pltpu.VMEM),
        scratch_shapes=[
            pltpu.VMEM((rows, samples), jnp.bfloat16),
            pltpu.VMEM(tabs.shape, jnp.bfloat16),
            pltpu.VMEM(tabs.shape, jnp.float32),
            pltpu.VMEM((APER, 1, rows), jnp.int32),
            pltpu.VMEM((1, tiles), jnp.int32),
            pltpu.VMEM((1, rows), jnp.int32),
            pltpu.VMEM((APER, tiles), jnp.int32),
            pltpu.VMEM((APER, tiles), jnp.float32),
            pltpu.VMEM((rows, LANES), jnp.int32),
            pltpu.VMEM((rows, LANES), jnp.bfloat16),
            pltpu.VMEM((LANES, stations), jnp.float32),
            pltpu.VMEM((2, groups, BW, stations), jnp.float32),
            pltpu.VMEM((stations, LANES), jnp.float32),
            pltpu.VMEM((stations, LANES), jnp.float32),
            pltpu.VMEM((2, 2 * cols, LANES), jnp.float32),
            pltpu.SemaphoreType.DMA((6,)),
            pltpu.SemaphoreType.DMA((CHUNKS,)),
            pltpu.SemaphoreType.DMA((NOFF,)),
            pltpu.SemaphoreType.DMA((2, groups)),
            pltpu.SemaphoreType.DMA((groups - 1,)),
            pltpu.SemaphoreType.DMA((groups,)),
        ],
        compiler_params=pltpu.CompilerParams(
            collective_id=0, has_side_effects=True, vmem_limit_bytes=60 * 1024 * 1024
        ),
        name="migrate",
    )(
        traces.reshape(rows, samples),
        tabs,
        band_start.reshape(APER, 1, rows),
        src_vtation.reshape(1, tiles),
        rec_station,
        aperture.T,
        aperture_weight.T,
    )
    return jnp.sum(parts, axis=0).reshape(1, points)


def solution(mesh):
    placed = (
        P("blk", "off", None, None),
        P("blk", None, None, None),
        P("blk", "off", None, None),
        P(),
        P(None, "off", None),
        P(),
        P(),
    )
    return jax.shard_map(
        shards, mesh=mesh, in_specs=placed, out_specs=P("blk", None), check_vma=False
    )
```

time: 483 us -> 31.9 us (0.07)
  other arithmetic: 339 us -> 1.36 us
  local copies, waits for them, and re-layouts: 46.7 us -> 0 us
  starting transfers between devices: 30.9 us -> 0 us
  Pallas kernels: 0 us -> 30.4 us
  matrix products: 29 us -> 0 us
  waiting for transfers between devices: 16.3 us -> 0 us
  blocking collectives: 11.3 us -> 0 us
  between operations: 6.52 us -> 0.01 us
    reduce_sum x11 -> x1, other arithmetic: 325 us -> 1.36 us  [shards(): return jnp.sum(parts, axis=0).reshape(1, points)]
    ppermute x12 -> x0, starting transfers between devices: 30.9 us -> none  [shifted(): lax.ppermute(x, axis, [(i, (i + by) % devices) for i in range(devices)])]
    pallas_call x0 -> x1, Pallas kernels: none -> 30.4 us  [shards(): pl.pallas_call(functools.partial(kernel, tiles, groups, scale), out_shape...]
    dot_general x5 -> x0, matrix products: 29 us -> none  [migrate(): jnp.dot(onehot, flat_table, preferred_element_type=jnp.float32)]
    slice x12 -> x0, local copies, waits for them, and re-layouts: 22.8 us -> none  [the longest x5 22 us: migrate(): samples[tap_number][:, None]]
    ppermute x12 -> x0, waiting for transfers between devices: 16.3 us -> none  [shifted(): lax.ppermute(x, axis, [(i, (i + by) % devices) for i in range(devices)])]
    unnamed x62 -> x0, local copies, waits for them, and re-layouts: 15.1 us -> none
    psum x1 -> x0, blocking collectives: 11.3 us -> none  [shards(): image_sum = lax.psum(accumulated, 'off') * norm_scale]
  transfers between devices with their start and end apart: 12 -> 0, of which waited for: 3 -> 0; matrix products, arithmetic and copies ran while one was open for 46% -> 0% of each run, Pallas kernels for 0% -> 0%
where the time goes in v1:
time: 31.9 us; the launch traced here: 31.8 us
  Pallas kernels  30.4 us (95%)
  other arithmetic  1.36 us (4%)
    pallas_call x1, Pallas kernels, shards(): pl.pallas_call(functools.partial(kernel, tiles, groups, scale), out_shape...  30.4 us
    reduce_sum x1, other arithmetic, shards(): return jnp.sum(parts, axis=0).reshape(1, points)  1.36 us

profile of v1, /device:TPU:1, one launch (start us, length us, event | category | flops | bytes accessed | tf_op | source)
XLA Modules:
  0.0 31.8 jit_solution(1581368085736947592)
XLA Ops:
  0.0 30.4 %migrate.1 = f32[4,16,128]{2,1,0:T(8,128)} custom-call(bf16[1024,2048]{1,0:T(8,128)(2,1)} %bitcast.11, bf16[4096,128]{1,0:T(8,128)(2,1)} %bitcast.12, s32[5,1,1024]{2,1,0:T(1,128)} %bitcast.13, s32[1,64]{1,0:T(1,128)} %bitcast.16, s32[64,1,1024]{2,1,0:T(1,128)} %rec.1, s32[5,64]{1,0:T(8,128)} %bitcast.14, f32[5,64]{1,0:T(8,128)} %bitcast.15), custom_call_target="tpu_custom_call" | custom-call | tf_op jit(solution)/shard_map/migrate/pallas_call | solution.py:272
  30.4 1.4 %reduce_sum.9 = f32[16,128]{1,0:T(8,128)} reduce(f32[4,16,128]{2,1,0:T(8,128)} %migrate.1, f32[]{:T(128)} %constant.0.clone.1), dimensions={0}, to_apply=%region_0.0 | reduce | flops 6144 | bytes 40964 | tf_op jit(solution)/shard_map/reduce_sum | solution.py:313

commit v2 on v1

--- a/solution.py
+++ b/solution.py
@@ -13,13 +13,24 @@
 HALF = 3
 NOFF = 2 * HALF + 1
 LANES = 128
-CHUNKS = 8
+CHUNKS = 4
 STEP = 16
+UNROLL = 16
 MESH = pl.DeviceIdType.MESH
 
 
 def lane_take(x, idx):
-    return jnp.take_along_axis(x, idx, axis=1, mode="promise_in_bounds")
+    numbers = lax.GatherDimensionNumbers(
+        offset_dims=(),
+        collapsed_slice_dims=(1,),
+        start_index_map=(1,),
+        operand_batching_dims=(0,),
+        start_indices_batching_dims=(0,),
+    )
+    return lax.gather(
+        x, idx[..., None], numbers, slice_sizes=(1, 1),
+        mode=lax.GatherScatterMode.PROMISE_IN_BOUNDS,
+    )
 
 
 def kernel(
@@ -27,7 +38,7 @@
     traces, tabs, starts, src, rec, aper, aw,
     out,
     trace_v, tabs_v, tab32, starts_v, src_v, rec_v, aper_v, aw_v,
-    pos_v, window_v, send_v, recv_v, low_v, slope_v, source_v,
+    pos_v, window_v, send_v, recv_v, table_v, source_v,
     load_sem, chunk_sem, send_sem, recv_sem, peer_send_sem, peer_recv_sem,
 ):
     rows, samples = trace_v.shape
@@ -92,33 +103,34 @@
         digits, pick, (((0,), (0,)), ((), ())), preferred_element_type=jnp.float32
     )
     tap = lax.broadcasted_iota(jnp.int32, (rows, LANES), 1) & (BW - 1)
-    pos_v[...] = first.astype(jnp.int32) + tap
-
-    def do_chunk(i, carry):
+    pos_v[...] = (first.astype(jnp.int32) + tap).astype(jnp.int16)
+
+    small[2].wait()
+    station_id = lax.broadcasted_iota(jnp.int32, (stations, per), 0)
+    sums = jnp.zeros((stations, LANES), jnp.float32)
+    for i in range(CHUNKS):
         chunk_copy(i).wait()
 
-        def do_rows(k, inner):
+        def do_rows(k, inner, i=i):
             span = pl.ds(pl.multiple_of(i * per + k * STEP, STEP), STEP)
             pos = pos_v[span, :]
-            inside = pos & (LANES - 1)
-            block = pos >> 7
-            acc = jnp.zeros((STEP, LANES), jnp.float32)
+            inside = pos & jnp.int16(LANES - 1)
+            block = pos >> jnp.int16(7)
+            acc = jnp.zeros((STEP, LANES), jnp.bfloat16)
             for c in range(samples // LANES):
-                piece = trace_v[span, c * LANES:(c + 1) * LANES].astype(jnp.float32)
-                acc = jnp.where(block == c, lane_take(piece, inside), acc)
-            window_v[span, :] = acc.astype(jnp.bfloat16)
+                piece = lane_take(trace_v[span, c * LANES:(c + 1) * LANES], inside)
+                acc = jnp.where(block == jnp.int16(c), piece, acc)
+            window_v[span, :] = acc
             return inner
 
-        return lax.fori_loop(0, per // STEP, do_rows, carry)
-
-    lax.fori_loop(0, CHUNKS, do_chunk, 0)
-
-    small[2].wait()
-    onehot = (
-        lax.broadcasted_iota(jnp.int32, (stations, rows), 0) == rec_v[...]
-    ).astype(jnp.float32).astype(jnp.bfloat16)
-    sums = jnp.dot(onehot, window_v[...], preferred_element_type=jnp.float32) * taper_row
-    send_v[...] = sums.T
+        lax.fori_loop(0, per // STEP, do_rows, 0, unroll=min(UNROLL, per // STEP))
+        onehot = (station_id == rec_v[:, i * per:(i + 1) * per]).astype(jnp.float32)
+        sums = sums + jnp.dot(
+            onehot.astype(jnp.bfloat16),
+            window_v[i * per:(i + 1) * per, :],
+            preferred_element_type=jnp.float32,
+        )
+    send_v[...] = (sums * taper_row).T
 
     pl.semaphore_wait(barrier, groups - 1 + 2 * HALF)
 
@@ -192,39 +204,42 @@
 
     base = []
     slope = []
-    tap_id = lax.broadcasted_iota(jnp.int32, (BW, stations), 0).astype(jnp.float32)
     for slot in range(2):
         total = (recv_v[slot, 0] + recv_v[slot, 1]) + (recv_v[slot, 2] + recv_v[slot, 3])
         after = jnp.concatenate([total[1:], total[BW - 1:]], axis=0)
-        step = after - total
-        base.append(total - tap_id * step)
-        slope.append(step)
-    rest = jnp.zeros((LANES - 2 * BW, stations), jnp.float32)
-    low_v[...] = jnp.concatenate(base + [rest], axis=0).T
-    slope_v[...] = jnp.concatenate(slope + [rest], axis=0).T
-
-    sources = [
-        (source_v[slot, pl.ds(0, cols, stride=2), :], source_v[slot, pl.ds(1, cols, stride=2), :])
-        for slot in range(2)
-    ]
-
-    def do_station(r, acc):
-        row = pl.multiple_of(r * (2 * cols), 2 * cols)
-        time = tab32[pl.ds(row, cols, stride=2), :]
-        amp = tab32[pl.ds(row + 1, cols, stride=2), :]
-        base_row = jnp.broadcast_to(low_v[pl.ds(r, 1), :], (cols, LANES))
-        slope_row = jnp.broadcast_to(slope_v[pl.ds(r, 1), :], (cols, LANES))
-        result = []
-        for slot in range(2):
-            arrival = sources[slot][0] + time
-            cell = arrival.astype(jnp.int32) + BW * slot
-            value = lane_take(base_row, cell) + lane_take(slope_row, cell) * arrival
-            result.append(acc[slot] + amp * value)
-        return tuple(result)
-
-    zero = jnp.zeros((cols, LANES), jnp.float32)
-    acc = lax.fori_loop(0, stations, do_station, (zero, zero), unroll=4)
-    out[off] = (sources[0][1] * acc[0] + sources[1][1] * acc[1]) * scale
+        base.append(total)
+        slope.append(after - total)
+    rest = jnp.zeros((LANES - 4 * BW, stations), jnp.float32)
+    both = jnp.concatenate(base + slope + [rest], axis=0).T
+    for n, table in enumerate((both, pltpu.roll(both, LANES - 2 * BW, 1))):
+        upper = table.astype(jnp.bfloat16)
+        table_v[2 * n] = upper
+        table_v[2 * n + 1] = (table - upper.astype(jnp.float32)).astype(jnp.bfloat16)
+
+    def do_column(c, carry):
+        time_at = [source_v[slot, pl.ds(2 * c, 1), :] for slot in range(2)]
+        amp_at = [source_v[slot, pl.ds(2 * c + 1, 1), :] for slot in range(2)]
+        acc = [jnp.zeros((STEP, LANES), jnp.float32) for slot in range(2)]
+        for first_station in range(0, stations, STEP):
+            row = first_station * 2 * cols + 2 * c
+            time = tab32[pl.ds(row, STEP, stride=2 * cols), :]
+            amp = tab32[pl.ds(row + 1, STEP, stride=2 * cols), :]
+            near = [table_v[n, first_station:first_station + STEP, :] for n in range(4)]
+            for slot in range(2):
+                arrival = time_at[slot] + time
+                whole = arrival.astype(jnp.int32)
+                part = arrival - whole.astype(jnp.float32)
+                cell = whole.astype(jnp.int16)
+                if slot:
+                    cell = cell + jnp.int16(BW)
+                got = [lane_take(x, cell).astype(jnp.float32) for x in near]
+                value = (got[0] + got[1]) + (got[2] + got[3]) * part
+                acc[slot] = acc[slot] + amp * value
+        both_acc = amp_at[0] * acc[0] + amp_at[1] * acc[1]
+        out[off, pl.ds(c, 1), :] = jnp.sum(both_acc, axis=0, keepdims=True) * scale
+        return carry
+
+    lax.fori_loop(0, cols, do_column, 0, unroll=2)
 
     def peer_copy(step):
         return pltpu.make_async_remote_copy(
@@ -283,12 +298,11 @@
             pltpu.VMEM((1, rows), jnp.int32),
             pltpu.VMEM((APER, tiles), jnp.int32),
             pltpu.VMEM((APER, tiles), jnp.float32),
-            pltpu.VMEM((rows, LANES), jnp.int32),
+            pltpu.VMEM((rows, LANES), jnp.int16),
             pltpu.VMEM((rows, LANES), jnp.bfloat16),
             pltpu.VMEM((LANES, stations), jnp.float32),
             pltpu.VMEM((2, groups, BW, stations), jnp.float32),
-            pltpu.VMEM((stations, LANES), jnp.float32),
-            pltpu.VMEM((stations, LANES), jnp.float32),
+            pltpu.VMEM((4, stations, LANES), jnp.bfloat16),
             pltpu.VMEM((2, 2 * cols, LANES), jnp.float32),
             pltpu.SemaphoreType.DMA((6,)),
             pltpu.SemaphoreType.DMA((CHUNKS,)),

time: 31.9 us -> 25.4 us (0.80)
  Pallas kernels: 30.4 us -> 23.9 us
    pallas_call x1, Pallas kernels: 30.4 us -> 23.9 us  [shards(): pl.pallas_call(functools.partial(kernel, tiles, groups, scale), out_shape...]
where the time goes in v2:
time: 25.4 us; the launch traced here: 25.2 us
  Pallas kernels  23.9 us (94%)
  other arithmetic  1.36 us (5%)
    pallas_call x1, Pallas kernels, shards(): pl.pallas_call(functools.partial(kernel, tiles, groups, scale), out_shape...  23.9 us
    reduce_sum x1, other arithmetic, shards(): return jnp.sum(parts, axis=0).reshape(1, points)  1.36 us

profile of v2, /device:TPU:1, one launch (start us, length us, event | category | flops | bytes accessed | tf_op | source)
XLA Modules:
  0.0 25.2 jit_solution(8760270324033376770)
XLA Ops:
  0.0 23.9 %migrate.1 = f32[4,16,128]{2,1,0:T(8,128)} custom-call(bf16[1024,2048]{1,0:T(8,128)(2,1)} %bitcast.11, bf16[4096,128]{1,0:T(8,128)(2,1)} %bitcast.12, s32[5,1,1024]{2,1,0:T(1,128)} %bitcast.13, s32[1,64]{1,0:T(1,128)} %bitcast.16, s32[64,1,1024]{2,1,0:T(1,128)} %rec.1, s32[5,64]{1,0:T(8,128)} %bitcast.14, f32[5,64]{1,0:T(8,128)} %bitcast.15), custom_call_target="tpu_custom_call" | custom-call | tf_op jit(solution)/shard_map/migrate/pallas_call | solution.py:287
  23.9 1.4 %reduce_sum.9 = f32[16,128]{1,0:T(8,128)} reduce(f32[4,16,128]{2,1,0:T(8,128)} %migrate.1, f32[]{:T(128)} %constant.0.clone.1), dimensions={0}, to_apply=%region_0.0 | reduce | flops 6144 | bytes 40964 | tf_op jit(solution)/shard_map/reduce_sum | solution.py:327

commit v3 on v2

--- a/solution.py
+++ b/solution.py
@@ -12,6 +12,10 @@
 APER = 5
 HALF = 3
 NOFF = 2 * HALF + 1
+CORES = 2
+SPLIT = 3
+TAKEN = ((-2, -1, 1, SPLIT), (0, -3, 2, SPLIT))
+SEND_ORDER = (3, 2, 1, 0, -1, -2, -3)
 LANES = 128
 CHUNKS = 4
 STEP = 16
@@ -38,7 +42,7 @@
     traces, tabs, starts, src, rec, aper, aw,
     out,
     trace_v, tabs_v, tab32, starts_v, src_v, rec_v, aper_v, aw_v,
-    pos_v, window_v, send_v, recv_v, table_v, source_v,
+    pos_v, window_v, send_v, recv_v, table_v, source_v, time_v, amp_v, early_v,
     load_sem, chunk_sem, send_sem, recv_sem, peer_send_sem, peer_recv_sem,
 ):
     rows, samples = trace_v.shape
@@ -49,18 +53,30 @@
     def at_tile(d):
         return lax.rem(blk + (d + tiles), tiles)
 
+    core = lax.rem(off, CORES)
+    chip_first = off - core
+    sibling = chip_first + (1 - core)
+
+    def taken(slot):
+        return jnp.where(core == 0, TAKEN[0][slot], TAKEN[1][slot])
+
     barrier = pltpu.get_barrier_semaphore()
-    for step in range(1, groups):
-        pl.semaphore_signal(
-            barrier, inc=1, device_id=(blk, lax.rem(off + step, groups)), device_id_type=MESH
-        )
-
-    @pl.when(off > 0)
-    def _():
-        for sign in (-1, 1):
-            for g in range(groups):
-                other = lax.rem(blk + sign * off + tiles, tiles)
-                pl.semaphore_signal(barrier, inc=1, device_id=(other, g), device_id_type=MESH)
+
+    def greet(tile, g):
+        pl.semaphore_signal(barrier, inc=1, device_id=(tile, g), device_id_type=MESH)
+
+    for c in range(CORES):
+        @pl.when(core == c)
+        def _(c=c):
+            for d in reversed(TAKEN[c]):
+                if d:
+                    for g in range(groups):
+                        greet(at_tile(-d), g)
+            if 0 in TAKEN[c]:
+                for step in range(1, groups):
+                    greet(blk, lax.rem(off + step, groups))
+            else:
+                greet(blk, sibling)
 
     small = [
         pltpu.make_async_copy(starts, starts_v, load_sem.at[0]),
@@ -132,17 +148,16 @@
         )
     send_v[...] = (sums * taper_row).T
 
-    pl.semaphore_wait(barrier, groups - 1 + 2 * HALF)
-
-    def band_copy(d):
-        slot = 1 if d > 0 else 0
-        o = d + HALF
+    chips = groups // CORES
+    pl.semaphore_wait(barrier, (NOFF + 1) * chips)
+
+    def band_copy(d, c, chip, number):
         return pltpu.make_async_remote_copy(
-            src_ref=send_v.at[pl.ds(o * BW, BW)],
-            dst_ref=recv_v.at[slot, off],
-            send_sem=send_sem.at[o],
-            recv_sem=recv_sem.at[slot, off],
-            device_id=(at_tile(d), abs(d)),
+            src_ref=send_v.at[pl.ds((d + HALF) * BW, BW)],
+            dst_ref=recv_v.at[TAKEN[c].index(d), off],
+            send_sem=send_sem.at[number],
+            recv_sem=recv_sem.at[TAKEN[c].index(d), off],
+            device_id=(at_tile(d), chip * CORES + c),
             device_id_type=MESH,
         )
 
@@ -152,26 +167,36 @@
             dst_ref=recv_v.at[slot, g],
             send_sem=send_sem.at[0],
             recv_sem=recv_sem.at[slot, g],
-            device_id=(blk, off),
+            device_id=(blk, sibling),
             device_id_type=MESH,
         ).wait_recv()
 
-    for d in (-3, 3, -2, 2, -1, 1):
-        band_copy(d).start()
-
-    @pl.when(off > 0)
+    outgoing = [
+        (d, c, chip)
+        for d in SEND_ORDER for c in range(CORES) if d in TAKEN[c] for chip in range(chips)
+    ]
+
+    def each_copy(act):
+        for number, (d, c, chip) in enumerate(outgoing):
+            copy = band_copy(d, c, chip, number)
+            if d == 0:
+                pl.when(off != chip * CORES + c)(functools.partial(act, copy))
+            else:
+                act(copy)
+
+    each_copy(lambda copy: copy.start())
+
+    home = TAKEN[1].index(0)
+
+    @pl.when(core == 1)
     def _():
-        band_copy(0).start()
-
-    @pl.when(off == 0)
-    def _():
-        recv_v[0, 0] = send_v[HALF * BW:(HALF + 1) * BW, :]
-        recv_v[1] = jnp.zeros(recv_v.shape[1:], jnp.float32)
+        recv_v[home, off] = send_v[HALF * BW:(HALF + 1) * BW, :]
 
     tabs_copy.wait()
     small[4].wait()
     cols = tab32.shape[0] // stations // 2
-    origins = (at_tile(off), lax.rem(blk - off + tiles, tiles))
+    slots = len(TAKEN[0])
+    origins = [lax.rem(blk - taken(slot) + tiles, tiles) for slot in range(slots)]
     lane = lax.broadcasted_iota(jnp.int32, (1, tiles), 1)
     source_ids = [
         jnp.sum(jnp.where(lane == origin, src_v[...], 0), axis=1, keepdims=True)
@@ -185,93 +210,105 @@
         return tuple(jnp.where(i == r, wide, old) for i, old in zip(source_ids, rows_of))
 
     blank = jnp.zeros((2 * cols, LANES), jnp.float32)
-    found = lax.fori_loop(0, stations, widen, (blank, blank), unroll=4)
-    source_v[0] = found[0]
-    source_v[1] = found[1]
-
-    for g in range(groups):
-        if g == 0:
-            @pl.when(off > 0)
-            def _():
-                band_wait(0, 0)
-        else:
-            band_wait(0, g)
-
-    @pl.when(off > 0)
-    def _():
-        for g in range(groups):
-            band_wait(1, g)
-
-    base = []
-    slope = []
-    for slot in range(2):
-        total = (recv_v[slot, 0] + recv_v[slot, 1]) + (recv_v[slot, 2] + recv_v[slot, 3])
-        after = jnp.concatenate([total[1:], total[BW - 1:]], axis=0)
-        base.append(total)
-        slope.append(after - total)
-    rest = jnp.zeros((LANES - 4 * BW, stations), jnp.float32)
-    both = jnp.concatenate(base + slope + [rest], axis=0).T
-    for n, table in enumerate((both, pltpu.roll(both, LANES - 2 * BW, 1))):
-        upper = table.astype(jnp.bfloat16)
-        table_v[2 * n] = upper
-        table_v[2 * n + 1] = (table - upper.astype(jnp.float32)).astype(jnp.bfloat16)
-
-    def do_column(c, carry):
-        time_at = [source_v[slot, pl.ds(2 * c, 1), :] for slot in range(2)]
-        amp_at = [source_v[slot, pl.ds(2 * c + 1, 1), :] for slot in range(2)]
-        acc = [jnp.zeros((STEP, LANES), jnp.float32) for slot in range(2)]
+    found = lax.fori_loop(0, stations, widen, (blank,) * slots, unroll=4)
+    for slot in range(slots):
+        source_v[slot] = found[slot]
+
+    def regroup(c, carry):
         for first_station in range(0, stations, STEP):
             row = first_station * 2 * cols + 2 * c
-            time = tab32[pl.ds(row, STEP, stride=2 * cols), :]
-            amp = tab32[pl.ds(row + 1, STEP, stride=2 * cols), :]
-            near = [table_v[n, first_station:first_station + STEP, :] for n in range(4)]
-            for slot in range(2):
-                arrival = time_at[slot] + time
+            time_v[c, first_station:first_station + STEP, :] = tab32[pl.ds(row, STEP, stride=2 * cols), :]
+            amp_v[c, first_station:first_station + STEP, :] = tab32[pl.ds(row + 1, STEP, stride=2 * cols), :]
+        return carry
+
+    lax.fori_loop(0, cols, regroup, 0)
+
+    def collect(pair):
+        base = []
+        slope = []
+        for slot in pair:
+            for g in range(groups):
+                if slot == home:
+                    @pl.when(jnp.logical_or(core == 0, off != g))
+                    def _(g=g):
+                        band_wait(slot, g)
+                else:
+                    band_wait(slot, g)
+            total = (recv_v[slot, 0] + recv_v[slot, 1]) + (recv_v[slot, 2] + recv_v[slot, 3])
+            after = jnp.concatenate([total[1:], total[BW - 1:]], axis=0)
+            base.append(total)
+            slope.append(after - total)
+        rest = jnp.zeros((LANES - 4 * BW, stations), jnp.float32)
+        both = jnp.concatenate(base + slope + [rest], axis=0).T
+        for n, table in enumerate((both, pltpu.roll(both, LANES - 2 * BW, 1))):
+            upper = table.astype(jnp.bfloat16)
+            table_v[2 * n] = upper
+            table_v[2 * n + 1] = (table - upper.astype(jnp.float32)).astype(jnp.bfloat16)
+
+    def column(c, first_slot, count):
+        acc = [jnp.zeros((STEP, LANES), jnp.float32) for _ in range(count)]
+        time_at = [source_v[first_slot + n, pl.ds(2 * c, 1), :] for n in range(count)]
+        amp_at = [source_v[first_slot + n, pl.ds(2 * c + 1, 1), :] for n in range(count)]
+        for first_station in range(0, stations, STEP):
+            span = slice(first_station, first_station + STEP)
+            time = time_v[c, span, :]
+            amp = amp_v[c, span, :]
+            near = [table_v[n, span, :] for n in range(4)]
+            for n in range(count):
+                arrival = time_at[n] + time
                 whole = arrival.astype(jnp.int32)
                 part = arrival - whole.astype(jnp.float32)
                 cell = whole.astype(jnp.int16)
-                if slot:
+                if n:
                     cell = cell + jnp.int16(BW)
                 got = [lane_take(x, cell).astype(jnp.float32) for x in near]
                 value = (got[0] + got[1]) + (got[2] + got[3]) * part
-                acc[slot] = acc[slot] + amp * value
-        both_acc = amp_at[0] * acc[0] + amp_at[1] * acc[1]
-        out[off, pl.ds(c, 1), :] = jnp.sum(both_acc, axis=0, keepdims=True) * scale
+                acc[n] = acc[n] + amp * value
+        whole_acc = amp_at[0] * acc[0]
+        for n in range(1, count):
+            whole_acc = whole_acc + amp_at[n] * acc[n]
+        return jnp.sum(whole_acc, axis=0, keepdims=True)
+
+    half = cols // CORES
+    mine_first = core * half
+    other_first = half - mine_first
+
+    def early(c, carry):
+        early_v[pl.ds(c, 1), :] = column(c, 0, 2)
         return carry
 
-    lax.fori_loop(0, cols, do_column, 0, unroll=2)
-
-    def peer_copy(step):
-        return pltpu.make_async_remote_copy(
-            src_ref=out.at[off],
-            dst_ref=out.at[off],
-            send_sem=peer_send_sem.at[step - 1],
-            recv_sem=peer_recv_sem.at[off],
-            device_id=(blk, lax.rem(off + step, groups)),
-            device_id_type=MESH,
-        )
-
-    for step in range(1, groups):
-        peer_copy(step).start()
-    for step in range(1, groups):
-        other = lax.rem(off + step, groups)
-        pltpu.make_async_remote_copy(
-            src_ref=out.at[off],
-            dst_ref=out.at[other],
-            send_sem=peer_send_sem.at[step - 1],
-            recv_sem=peer_recv_sem.at[other],
-            device_id=(blk, other),
-            device_id_type=MESH,
-        ).wait_recv()
-    for d in (-3, 3, -2, 2, -1, 1):
-        band_copy(d).wait_send()
-
-    @pl.when(off > 0)
-    def _():
-        band_copy(0).wait_send()
-
-    for step in range(1, groups):
-        peer_copy(step).wait_send()
+    def late(first, count):
+        def step(i, carry):
+            c = first + i
+            out[core, pl.ds(c, 1), :] = (early_v[pl.ds(c, 1), :] + column(c, 2, count)) * scale
+            return carry
+        return step
+
+    collect((0, 1))
+    lax.fori_loop(0, cols, early, 0, unroll=2)
+    collect((2, 3))
+    lax.fori_loop(0, half, late(mine_first, 2), 0, unroll=2)
+    lax.fori_loop(0, half, late(other_first, 1), 0, unroll=2)
+
+    exchange = pltpu.make_async_remote_copy(
+        src_ref=out.at[core],
+        dst_ref=out.at[core],
+        send_sem=peer_send_sem,
+        recv_sem=peer_recv_sem,
+        device_id=(blk, sibling),
+        device_id_type=MESH,
+    )
+    exchange.start()
+    pltpu.make_async_remote_copy(
+        src_ref=out.at[core],
+        dst_ref=out.at[1 - core],
+        send_sem=peer_send_sem,
+        recv_sem=peer_recv_sem,
+        device_id=(blk, sibling),
+        device_id_type=MESH,
+    ).wait_recv()
+    each_copy(lambda copy: copy.wait_send())
+    exchange.wait_send()
 
 
 def shards(traces, tables, band_start, src_vtation, rec_station, aperture, aperture_weight):
@@ -286,7 +323,7 @@
     any_spec = pl.BlockSpec(memory_space=pltpu.HBM)
     parts = pl.pallas_call(
         functools.partial(kernel, tiles, groups, scale),
-        out_shape=jax.ShapeDtypeStruct((groups, cols, LANES), jnp.float32),
+        out_shape=pltpu.VMEM((CORES, cols, LANES), jnp.float32),
         in_specs=[any_spec] * 7,
         out_specs=pl.BlockSpec(memory_space=pltpu.VMEM),
         scratch_shapes=[
@@ -301,15 +338,18 @@
             pltpu.VMEM((rows, LANES), jnp.int16),
             pltpu.VMEM((rows, LANES), jnp.bfloat16),
             pltpu.VMEM((LANES, stations), jnp.float32),
-            pltpu.VMEM((2, groups, BW, stations), jnp.float32),
+            pltpu.VMEM((len(TAKEN[0]), groups, BW, stations), jnp.float32),
             pltpu.VMEM((4, stations, LANES), jnp.bfloat16),
-            pltpu.VMEM((2, 2 * cols, LANES), jnp.float32),
+            pltpu.VMEM((len(TAKEN[0]), 2 * cols, LANES), jnp.float32),
+            pltpu.VMEM((cols, stations, LANES), jnp.float32),
+            pltpu.VMEM((cols, stations, LANES), jnp.float32),
+            pltpu.VMEM((cols, LANES), jnp.float32),
             pltpu.SemaphoreType.DMA((6,)),
             pltpu.SemaphoreType.DMA((CHUNKS,)),
-            pltpu.SemaphoreType.DMA((NOFF,)),
-            pltpu.SemaphoreType.DMA((2, groups)),
-            pltpu.SemaphoreType.DMA((groups - 1,)),
-            pltpu.SemaphoreType.DMA((groups,)),
+            pltpu.SemaphoreType.DMA(((NOFF + 1) * groups // CORES,)),
+            pltpu.SemaphoreType.DMA((len(TAKEN[0]), groups)),
+            pltpu.SemaphoreType.DMA,
+            pltpu.SemaphoreType.DMA,
         ],
         compiler_params=pltpu.CompilerParams(
             collective_id=0, has_side_effects=True, vmem_limit_bytes=60 * 1024 * 1024

time: 25.4 us -> 22.5 us (0.89)
  Pallas kernels: 23.9 us -> 21.8 us
  other arithmetic: 1.36 us -> 0.6 us
    pallas_call x1, Pallas kernels: 23.9 us -> 21.8 us  [shards(): pl.pallas_call(functools.partial(kernel, tiles, groups, scale), out_shape...]
    reduce_sum x1, other arithmetic: 1.36 us -> 0.6 us  [shards(): return jnp.sum(parts, axis=0).reshape(1, points)]
where the time goes in v3:
time: 22.5 us; the launch traced here: 22.4 us
  Pallas kernels  21.8 us (97%)
  other arithmetic  0.6 us (3%)
    pallas_call x1, Pallas kernels, shards(): pl.pallas_call(functools.partial(kernel, tiles, groups, scale), out_shape...  21.8 us
    reduce_sum x1, other arithmetic, shards(): return jnp.sum(parts, axis=0).reshape(1, points)  0.6 us

profile of v3, /device:TPU:1, one launch (start us, length us, event | category | flops | bytes accessed | tf_op | source)
XLA Modules:
  0.0 22.4 jit_solution(10597415101751063338)
XLA Ops:
  0.0 21.8 %migrate.1 = f32[2,16,128]{2,1,0:T(8,128)S(1)} custom-call(bf16[1024,2048]{1,0:T(8,128)(2,1)} %bitcast.11, bf16[4096,128]{1,0:T(8,128)(2,1)} %bitcast.12, s32[5,1,1024]{2,1,0:T(1,128)} %bitcast.13, s32[1,64]{1,0:T(1,128)} %bitcast.16, s32[64,1,1024]{2,1,0:T(1,128)} %rec.1, s32[5,64]{1,0:T(8,128)} %bitcast.14, f32[5,64]{1,0:T(8,128)} %bitcast.15), custom_call_target="tpu_custom_call" | custom-call | tf_op jit(solution)/shard_map/migrate/pallas_call | solution.py:324
  21.8 0.6 %reduce_sum.9 = f32[16,128]{1,0:T(8,128)} reduce(f32[2,16,128]{2,1,0:T(8,128)S(1)} %migrate.1, f32[]{:T(128)} %constant.0.clone.1), dimensions={0}, to_apply=%region_0.0 | reduce | flops 2048 | bytes 24580 | tf_op jit(solution)/shard_map/reduce_sum | solution.py:367

commit v4 on v3

--- a/solution.py
+++ b/solution.py
@@ -42,8 +42,8 @@
     traces, tabs, starts, src, rec, aper, aw,
     out,
     trace_v, tabs_v, tab32, starts_v, src_v, rec_v, aper_v, aw_v,
-    pos_v, window_v, send_v, recv_v, table_v, source_v, time_v, amp_v, early_v,
-    load_sem, chunk_sem, send_sem, recv_sem, peer_send_sem, peer_recv_sem,
+    pos_v, window_v, onehot_v, send_v, recv_v, table_v, source_v, time_v, amp_v, early_v,
+    load_sem, chunk_sem, send_sem, recv_sem, peer_send_sem, peer_recv_sem, ready_sem,
 ):
     rows, samples = trace_v.shape
     stations = send_v.shape[1]
@@ -52,31 +52,6 @@
 
     def at_tile(d):
         return lax.rem(blk + (d + tiles), tiles)
-
-    core = lax.rem(off, CORES)
-    chip_first = off - core
-    sibling = chip_first + (1 - core)
-
-    def taken(slot):
-        return jnp.where(core == 0, TAKEN[0][slot], TAKEN[1][slot])
-
-    barrier = pltpu.get_barrier_semaphore()
-
-    def greet(tile, g):
-        pl.semaphore_signal(barrier, inc=1, device_id=(tile, g), device_id_type=MESH)
-
-    for c in range(CORES):
-        @pl.when(core == c)
-        def _(c=c):
-            for d in reversed(TAKEN[c]):
-                if d:
-                    for g in range(groups):
-                        greet(at_tile(-d), g)
-            if 0 in TAKEN[c]:
-                for step in range(1, groups):
-                    greet(blk, lax.rem(off + step, groups))
-            else:
-                greet(blk, sibling)
 
     small = [
         pltpu.make_async_copy(starts, starts_v, load_sem.at[0]),
@@ -97,6 +72,65 @@
         chunk_copy(i).start()
     tabs_copy = pltpu.make_async_copy(tabs, tabs_v, load_sem.at[5])
     tabs_copy.start()
+
+    core = lax.rem(off, CORES)
+    chip_first = off - core
+    sibling = chip_first + (1 - core)
+
+    def taken(slot):
+        return jnp.where(core == 0, TAKEN[0][slot], TAKEN[1][slot])
+
+    barrier = pltpu.get_barrier_semaphore()
+
+    def greet(tile, g):
+        pl.semaphore_signal(barrier, inc=1, device_id=(tile, g), device_id_type=MESH)
+
+    for c in range(CORES):
+        @pl.when(core == c)
+        def _(c=c):
+            for d in reversed(TAKEN[c]):
+                if d > 0:
+                    for g in range(groups):
+                        greet(at_tile(-d), g)
+                elif d < 0:
+                    @pl.when(blk - d < tiles)
+                    def _(d=d):
+                        for g in range(groups):
+                            greet(at_tile(-d), g)
+            if 0 in TAKEN[c]:
+                for step in range(1, groups):
+                    greet(blk, lax.rem(off + step, groups))
+            else:
+                greet(blk, sibling)
+
+    chips = groups // CORES
+    for c in range(CORES):
+        for d in TAKEN[c]:
+            if d < 0:
+                @pl.when(blk + d < 0)
+                def _(c=c, d=d):
+                    for chip in range(chips):
+                        greet(at_tile(d), chip * CORES + c)
+
+    wraps_out = sum((blk + d < 0).astype(jnp.int32) for d in range(-HALF, 0))
+    wraps_in = sum(
+        jnp.logical_and(blk - d >= tiles, core == c).astype(jnp.int32)
+        for c in range(CORES) for d in TAKEN[c] if d < 0
+    )
+
+    def enter():
+        pl.semaphore_wait(barrier, (NOFF + 1) * chips - wraps_out * chips + wraps_in * groups)
+
+    def answer():
+        for c in range(CORES):
+            for d in TAKEN[c]:
+                if d < 0:
+                    @pl.when(jnp.logical_and(blk - d >= tiles, core == c))
+                    def _(d=d):
+                        for g in range(groups):
+                            pl.semaphore_signal(
+                                ready_sem, inc=1, device_id=(at_tile(-d), g), device_id_type=MESH
+                            )
 
     small[0].wait()
     small[1].wait()
@@ -122,10 +156,17 @@
     pos_v[...] = (first.astype(jnp.int32) + tap).astype(jnp.int16)
 
     small[2].wait()
-    station_id = lax.broadcasted_iota(jnp.int32, (stations, per), 0)
-    sums = jnp.zeros((stations, LANES), jnp.float32)
+    onehot = (
+        lax.broadcasted_iota(jnp.int32, (stations, rows), 0) == rec_v[...]
+    ).astype(jnp.float32).astype(jnp.bfloat16)
+    onehot_v[...] = onehot
     for i in range(CHUNKS):
         chunk_copy(i).wait()
+        if i == CHUNKS - 1:
+            @pl.when(wraps_in > 0)
+            def _():
+                enter()
+                answer()
 
         def do_rows(k, inner, i=i):
             span = pl.ds(pl.multiple_of(i * per + k * STEP, STEP), STEP)
@@ -140,16 +181,12 @@
             return inner
 
         lax.fori_loop(0, per // STEP, do_rows, 0, unroll=min(UNROLL, per // STEP))
-        onehot = (station_id == rec_v[:, i * per:(i + 1) * per]).astype(jnp.float32)
-        sums = sums + jnp.dot(
-            onehot.astype(jnp.bfloat16),
-            window_v[i * per:(i + 1) * per, :],
-            preferred_element_type=jnp.float32,
-        )
+    sums = jnp.dot(onehot_v[...], window_v[...], preferred_element_type=jnp.float32)
     send_v[...] = (sums * taper_row).T
 
-    chips = groups // CORES
-    pl.semaphore_wait(barrier, (NOFF + 1) * chips)
+    @pl.when(wraps_in == 0)
+    def _():
+        enter()
 
     def band_copy(d, c, chip, number):
         return pltpu.make_async_remote_copy(
@@ -184,8 +221,25 @@
             else:
                 act(copy)
 
-    each_copy(lambda copy: copy.start())
-
+    def start_straight():
+        for number, (d, c, chip) in enumerate(outgoing):
+            copy = band_copy(d, c, chip, number)
+            if d < 0:
+                pl.when(blk + d >= 0)(copy.start)
+            elif d == 0:
+                pl.when(off != chip * CORES + c)(copy.start)
+            else:
+                copy.start()
+
+    def start_wrapped():
+        @pl.when(wraps_out > 0)
+        def _():
+            pl.semaphore_wait(ready_sem, wraps_out * chips)
+            for number, (d, c, chip) in enumerate(outgoing):
+                if d < 0:
+                    pl.when(blk + d < 0)(band_copy(d, c, chip, number).start)
+
+    start_straight()
     home = TAKEN[1].index(0)
 
     @pl.when(core == 1)
@@ -286,9 +340,10 @@
 
     collect((0, 1))
     lax.fori_loop(0, cols, early, 0, unroll=2)
+    start_wrapped()
     collect((2, 3))
-    lax.fori_loop(0, half, late(mine_first, 2), 0, unroll=2)
-    lax.fori_loop(0, half, late(other_first, 1), 0, unroll=2)
+    lax.fori_loop(0, half, late(mine_first, 2), 0, unroll=8)
+    lax.fori_loop(0, half, late(other_first, 1), 0, unroll=8)
 
     exchange = pltpu.make_async_remote_copy(
         src_ref=out.at[core],
@@ -337,6 +392,7 @@
             pltpu.VMEM((APER, tiles), jnp.float32),
             pltpu.VMEM((rows, LANES), jnp.int16),
             pltpu.VMEM((rows, LANES), jnp.bfloat16),
+            pltpu.VMEM((stations, rows), jnp.bfloat16),
             pltpu.VMEM((LANES, stations), jnp.float32),
             pltpu.VMEM((len(TAKEN[0]), groups, BW, stations), jnp.float32),
             pltpu.VMEM((4, stations, LANES), jnp.bfloat16),
@@ -350,6 +406,7 @@
             pltpu.SemaphoreType.DMA((len(TAKEN[0]), groups)),
             pltpu.SemaphoreType.DMA,
             pltpu.SemaphoreType.DMA,
+            pltpu.SemaphoreType.REGULAR,
         ],
         compiler_params=pltpu.CompilerParams(
             collective_id=0, has_side_effects=True, vmem_limit_bytes=60 * 1024 * 1024

time: 22.5 us -> 21.1 us (0.938)
  Pallas kernels: 21.8 us -> 20.4 us
    pallas_call x1, Pallas kernels: 21.8 us -> 20.4 us  [shards(): pl.pallas_call(functools.partial(kernel, tiles, groups, scale), out_shape...]
where the time goes in v4:
time: 21.1 us
  Pallas kernels  20.4 us (97%)
  other arithmetic  0.6 us (3%)
    pallas_call x1, Pallas kernels, shards(): pl.pallas_call(functools.partial(kernel, tiles, groups, scale), out_shape...  20.4 us
    reduce_sum x1, other arithmetic, shards(): return jnp.sum(parts, axis=0).reshape(1, points)  0.6 us

profile of v4, /device:TPU:1, one launch (start us, length us, event | category | flops | bytes accessed | tf_op | source)
XLA Modules:
  0.0 21.1 jit_solution(4179217463353264568)
XLA Ops:
  0.0 20.4 %migrate.1 = f32[2,16,128]{2,1,0:T(8,128)S(1)} custom-call(bf16[1024,2048]{1,0:T(8,128)(2,1)} %bitcast.11, bf16[4096,128]{1,0:T(8,128)(2,1)} %bitcast.12, s32[5,1,1024]{2,1,0:T(1,128)} %bitcast.13, s32[1,64]{1,0:T(1,128)} %bitcast.16, s32[64,1,1024]{2,1,0:T(1,128)} %rec.1, s32[5,64]{1,0:T(8,128)} %bitcast.14, f32[5,64]{1,0:T(8,128)} %bitcast.15), custom_call_target="tpu_custom_call" | custom-call | tf_op jit(solution)/shard_map/migrate/pallas_call | solution.py:379
  20.5 0.6 %reduce_sum.9 = f32[16,128]{1,0:T(8,128)} reduce(f32[2,16,128]{2,1,0:T(8,128)S(1)} %migrate.1, f32[]{:T(128)} %constant.0.clone.1), dimensions={0}, to_apply=%region_0.0 | reduce | flops 2048 | bytes 24580 | tf_op jit(solution)/shard_map/reduce_sum | solution.py:424

commit v5 on v4

--- a/solution.py
+++ b/solution.py
@@ -14,6 +14,7 @@
 NOFF = 2 * HALF + 1
 CORES = 2
 SPLIT = 3
+SHARE = 6
 TAKEN = ((-2, -1, 1, SPLIT), (0, -3, 2, SPLIT))
 SEND_ORDER = (3, 2, 1, 0, -1, -2, -3)
 LANES = 128
@@ -212,6 +213,7 @@
         (d, c, chip)
         for d in SEND_ORDER for c in range(CORES) if d in TAKEN[c] for chip in range(chips)
     ]
+    outgoing.sort(key=lambda entry: (entry[0] <= 0, entry[1]))
 
     def each_copy(act):
         for number, (d, c, chip) in enumerate(outgoing):
@@ -323,10 +325,6 @@
             whole_acc = whole_acc + amp_at[n] * acc[n]
         return jnp.sum(whole_acc, axis=0, keepdims=True)
 
-    half = cols // CORES
-    mine_first = core * half
-    other_first = half - mine_first
-
     def early(c, carry):
         early_v[pl.ds(c, 1), :] = column(c, 0, 2)
         return carry
@@ -342,8 +340,13 @@
     lax.fori_loop(0, cols, early, 0, unroll=2)
     start_wrapped()
     collect((2, 3))
-    lax.fori_loop(0, half, late(mine_first, 2), 0, unroll=8)
-    lax.fori_loop(0, half, late(other_first, 1), 0, unroll=8)
+    for c in range(CORES):
+        @pl.when(core == c)
+        def _(c=c):
+            whole = (0, SHARE) if c == 0 else (SHARE, cols)
+            rest = (SHARE, cols) if c == 0 else (0, SHARE)
+            for (first, last), count in ((whole, 2), (rest, 1)):
+                lax.fori_loop(0, last - first, late(first, count), 0, unroll=last - first)
 
     exchange = pltpu.make_async_remote_copy(
         src_ref=out.at[core],

time: 21.1 us -> 20.7 us (0.981)
  Pallas kernels: 20.4 us -> 20 us
    pallas_call x1, Pallas kernels: 20.4 us -> 20 us  [shards(): pl.pallas_call(functools.partial(kernel, tiles, groups, scale), out_shape...]
where the time goes in v5:
time: 20.7 us; the launch traced here: 20.6 us
  Pallas kernels  20 us (97%)
  other arithmetic  0.6 us (3%)
    pallas_call x1, Pallas kernels, shards(): pl.pallas_call(functools.partial(kernel, tiles, groups, scale), out_shape...  20 us
    reduce_sum x1, other arithmetic, shards(): return jnp.sum(parts, axis=0).reshape(1, points)  0.6 us

profile of v5, /device:TPU:1, one launch (start us, length us, event | category | flops | bytes accessed | tf_op | source)
XLA Modules:
  0.0 20.6 jit_solution(11648658981615906895)
XLA Ops:
  0.0 20.0 %migrate.1 = f32[2,16,128]{2,1,0:T(8,128)S(1)} custom-call(bf16[1024,2048]{1,0:T(8,128)(2,1)} %bitcast.11, bf16[4096,128]{1,0:T(8,128)(2,1)} %bitcast.12, s32[5,1,1024]{2,1,0:T(1,128)} %bitcast.13, s32[1,64]{1,0:T(1,128)} %bitcast.16, s32[64,1,1024]{2,1,0:T(1,128)} %rec.1, s32[5,64]{1,0:T(8,128)} %bitcast.14, f32[5,64]{1,0:T(8,128)} %bitcast.15), custom_call_target="tpu_custom_call" | custom-call | tf_op jit(solution)/shard_map/migrate/pallas_call | solution.py:382
  20.0 0.6 %reduce_sum.9 = f32[16,128]{1,0:T(8,128)} reduce(f32[2,16,128]{2,1,0:T(8,128)S(1)} %migrate.1, f32[]{:T(128)} %constant.0.clone.1), dimensions={0}, to_apply=%region_0.0 | reduce | flops 2048 | bytes 24580 | tf_op jit(solution)/shard_map/reduce_sum | solution.py:427

commit v6 on v5

--- a/solution.py
+++ b/solution.py
@@ -43,7 +43,7 @@
     traces, tabs, starts, src, rec, aper, aw,
     out,
     trace_v, tabs_v, tab32, starts_v, src_v, rec_v, aper_v, aw_v,
-    pos_v, window_v, onehot_v, send_v, recv_v, table_v, source_v, time_v, amp_v, early_v,
+    pos_v, window_v, onehot_v, send_v, recv_v, table_v, flip_v, source_v, time_v, amp_v, early_v,
     load_sem, chunk_sem, send_sem, recv_sem, peer_send_sem, peer_recv_sem, ready_sem,
 ):
     rows, samples = trace_v.shape
@@ -61,15 +61,18 @@
         pltpu.make_async_copy(aw, aw_v, load_sem.at[3]),
         pltpu.make_async_copy(src, src_v, load_sem.at[4]),
     ]
-    for copy in small:
-        copy.start()
+    small[0].start()
+    small[1].start()
     per = rows // CHUNKS
 
     def chunk_copy(i):
         span = pl.ds(pl.multiple_of(i * per, per), per)
         return pltpu.make_async_copy(traces.at[span], trace_v.at[span], chunk_sem.at[i])
 
-    for i in range(CHUNKS):
+    chunk_copy(0).start()
+    for copy in small[2:]:
+        copy.start()
+    for i in range(1, CHUNKS):
         chunk_copy(i).start()
     tabs_copy = pltpu.make_async_copy(tabs, tabs_v, load_sem.at[5])
     tabs_copy.start()
@@ -135,14 +138,11 @@
 
     small[0].wait()
     small[1].wait()
-    small[3].wait()
     mine = lax.broadcasted_iota(jnp.int32, (APER, tiles), 1) == blk
     target = jnp.sum(jnp.where(mine, aper_v[...], 0), axis=1, keepdims=True)
-    taper = jnp.sum(jnp.where(mine, aw_v[...], 0.0), axis=1, keepdims=True)
     place = lax.rem(target - blk + (HALF + tiles), tiles)
     lane_off = lax.broadcasted_iota(jnp.int32, (APER, LANES), 1) // BW
     hit = (lane_off == place).astype(jnp.float32)
-    taper_row = jnp.sum(hit * taper, axis=0, keepdims=True)
     begin = starts_v[:, 0, :]
     high = (begin >> 7).astype(jnp.float32)
     low = (begin & (LANES - 1)).astype(jnp.float32)
@@ -157,6 +157,9 @@
     pos_v[...] = (first.astype(jnp.int32) + tap).astype(jnp.int16)
 
     small[2].wait()
+    small[3].wait()
+    taper = jnp.sum(jnp.where(mine, aw_v[...], 0.0), axis=1, keepdims=True)
+    taper_row = jnp.sum(hit * taper, axis=0, keepdims=True)
     onehot = (
         lax.broadcasted_iota(jnp.int32, (stations, rows), 0) == rec_v[...]
     ).astype(jnp.float32).astype(jnp.bfloat16)
@@ -248,9 +251,10 @@
     def _():
         recv_v[home, off] = send_v[HALF * BW:(HALF + 1) * BW, :]
 
+    flip_v[...] = jnp.zeros(flip_v.shape, jnp.float32)
     tabs_copy.wait()
     small[4].wait()
-    cols = tab32.shape[0] // stations // 2
+    cols = tabs_v.shape[0] // stations // 2
     slots = len(TAKEN[0])
     origins = [lax.rem(blk - taken(slot) + tiles, tiles) for slot in range(slots)]
     lane = lax.broadcasted_iota(jnp.int32, (1, tiles), 1)
@@ -280,8 +284,7 @@
     lax.fori_loop(0, cols, regroup, 0)
 
     def collect(pair):
-        base = []
-        slope = []
+        totals = []
         for slot in pair:
             for g in range(groups):
                 if slot == home:
@@ -290,13 +293,11 @@
                         band_wait(slot, g)
                 else:
                     band_wait(slot, g)
-            total = (recv_v[slot, 0] + recv_v[slot, 1]) + (recv_v[slot, 2] + recv_v[slot, 3])
-            after = jnp.concatenate([total[1:], total[BW - 1:]], axis=0)
-            base.append(total)
-            slope.append(after - total)
-        rest = jnp.zeros((LANES - 4 * BW, stations), jnp.float32)
-        both = jnp.concatenate(base + slope + [rest], axis=0).T
-        for n, table in enumerate((both, pltpu.roll(both, LANES - 2 * BW, 1))):
+            totals.append((recv_v[slot, 0] + recv_v[slot, 1]) + (recv_v[slot, 2] + recv_v[slot, 3]))
+        flip_v[:, 0:2 * BW] = jnp.concatenate(totals, axis=0).T
+        level = flip_v[...]
+        step = pltpu.roll(level, LANES - 1, 1) - level
+        for n, table in enumerate((level, step)):
             upper = table.astype(jnp.bfloat16)
             table_v[2 * n] = upper
             table_v[2 * n + 1] = (table - upper.astype(jnp.float32)).astype(jnp.bfloat16)
@@ -337,7 +338,7 @@
         return step
 
     collect((0, 1))
-    lax.fori_loop(0, cols, early, 0, unroll=2)
+    lax.fori_loop(0, cols, early, 0, unroll=4)
     start_wrapped()
     collect((2, 3))
     for c in range(CORES):
@@ -387,7 +388,7 @@
         scratch_shapes=[
             pltpu.VMEM((rows, samples), jnp.bfloat16),
             pltpu.VMEM(tabs.shape, jnp.bfloat16),
-            pltpu.VMEM(tabs.shape, jnp.float32),
+            pltpu.VMEM((tabs.shape[0] + 2 * cols, LANES), jnp.float32),
             pltpu.VMEM((APER, 1, rows), jnp.int32),
             pltpu.VMEM((1, tiles), jnp.int32),
             pltpu.VMEM((1, rows), jnp.int32),
@@ -399,6 +400,7 @@
             pltpu.VMEM((LANES, stations), jnp.float32),
             pltpu.VMEM((len(TAKEN[0]), groups, BW, stations), jnp.float32),
             pltpu.VMEM((4, stations, LANES), jnp.bfloat16),
+            pltpu.VMEM((stations, LANES), jnp.float32),
             pltpu.VMEM((len(TAKEN[0]), 2 * cols, LANES), jnp.float32),
             pltpu.VMEM((cols, stations, LANES), jnp.float32),
             pltpu.VMEM((cols, stations, LANES), jnp.float32),

time: 20.7 us -> 20.5 us (level)
  no operation moved by 1% of the time
where the time goes in v6:
time: 20.5 us
  Pallas kernels  19.9 us (97%)
  other arithmetic  0.6 us (3%)
    pallas_call x1, Pallas kernels, shards(): pl.pallas_call(functools.partial(kernel, tiles, groups, scale), out_shape...  19.9 us
    reduce_sum x1, other arithmetic, shards(): return jnp.sum(parts, axis=0).reshape(1, points)  0.6 us

profile of v6, /device:TPU:1, one launch (start us, length us, event | category | flops | bytes accessed | tf_op | source)
XLA Modules:
  0.0 20.5 jit_solution(5130350116173972203)
XLA Ops:
  0.0 19.9 %migrate.1 = f32[2,16,128]{2,1,0:T(8,128)S(1)} custom-call(bf16[1024,2048]{1,0:T(8,128)(2,1)} %bitcast.11, bf16[4096,128]{1,0:T(8,128)(2,1)} %bitcast.12, s32[5,1,1024]{2,1,0:T(1,128)} %bitcast.13, s32[1,64]{1,0:T(1,128)} %bitcast.16, s32[64,1,1024]{2,1,0:T(1,128)} %rec.1, s32[5,64]{1,0:T(8,128)} %bitcast.14, f32[5,64]{1,0:T(8,128)} %bitcast.15), custom_call_target="tpu_custom_call" | custom-call | tf_op jit(solution)/shard_map/migrate/pallas_call | solution.py:383
  19.9 0.6 %reduce_sum.9 = f32[16,128]{1,0:T(8,128)} reduce(f32[2,16,128]{2,1,0:T(8,128)S(1)} %migrate.1, f32[]{:T(128)} %constant.0.clone.1), dimensions={0}, to_apply=%region_0.0 | reduce | flops 2048 | bytes 24580 | tf_op jit(solution)/shard_map/reduce_sum | solution.py:429

commit v7 on v6

--- a/solution.py
+++ b/solution.py
@@ -157,9 +157,6 @@
     pos_v[...] = (first.astype(jnp.int32) + tap).astype(jnp.int16)
 
     small[2].wait()
-    small[3].wait()
-    taper = jnp.sum(jnp.where(mine, aw_v[...], 0.0), axis=1, keepdims=True)
-    taper_row = jnp.sum(hit * taper, axis=0, keepdims=True)
     onehot = (
         lax.broadcasted_iota(jnp.int32, (stations, rows), 0) == rec_v[...]
     ).astype(jnp.float32).astype(jnp.bfloat16)
@@ -185,6 +182,9 @@
             return inner
 
         lax.fori_loop(0, per // STEP, do_rows, 0, unroll=min(UNROLL, per // STEP))
+    small[3].wait()
+    taper = jnp.sum(jnp.where(mine, aw_v[...], 0.0), axis=1, keepdims=True)
+    taper_row = jnp.sum(hit * taper, axis=0, keepdims=True)
     sums = jnp.dot(onehot_v[...], window_v[...], preferred_element_type=jnp.float32)
     send_v[...] = (sums * taper_row).T
 
@@ -338,7 +338,7 @@
         return step
 
     collect((0, 1))
-    lax.fori_loop(0, cols, early, 0, unroll=4)
+    lax.fori_loop(0, cols, early, 0, unroll=8)
     start_wrapped()
     collect((2, 3))
     for c in range(CORES):

time: 20.5 us -> 20.5 us (level)
  no operation moved by 1% of the time
where the time goes in v7:
time: 20.5 us; the launch traced here: 20.4 us
  Pallas kernels  19.8 us (97%)
  other arithmetic  0.6 us (3%)
    pallas_call x1, Pallas kernels, shards(): pl.pallas_call(functools.partial(kernel, tiles, groups, scale), out_shape...  19.8 us
    reduce_sum x1, other arithmetic, shards(): return jnp.sum(parts, axis=0).reshape(1, points)  0.6 us

profile of v7, /device:TPU:1, one launch (start us, length us, event | category | flops | bytes accessed | tf_op | source)
XLA Modules:
  0.0 20.4 jit_solution(13991563266849591577)
XLA Ops:
  0.0 19.8 %migrate.1 = f32[2,16,128]{2,1,0:T(8,128)S(1)} custom-call(bf16[1024,2048]{1,0:T(8,128)(2,1)} %bitcast.11, bf16[4096,128]{1,0:T(8,128)(2,1)} %bitcast.12, s32[5,1,1024]{2,1,0:T(1,128)} %bitcast.13, s32[1,64]{1,0:T(1,128)} %bitcast.16, s32[64,1,1024]{2,1,0:T(1,128)} %rec.1, s32[5,64]{1,0:T(8,128)} %bitcast.14, f32[5,64]{1,0:T(8,128)} %bitcast.15), custom_call_target="tpu_custom_call" | custom-call | tf_op jit(solution)/shard_map/migrate/pallas_call | solution.py:383
  19.8 0.6 %reduce_sum.9 = f32[16,128]{1,0:T(8,128)} reduce(f32[2,16,128]{2,1,0:T(8,128)S(1)} %migrate.1, f32[]{:T(128)} %constant.0.clone.1), dimensions={0}, to_apply=%region_0.0 | reduce | flops 2048 | bytes 24580 | tf_op jit(solution)/shard_map/reduce_sum | solution.py:429
